TPU v7x, 128 devices: a whole 4x4x4 slice. The times are simulated.
128 devices in a mesh: dir: 32 (over x, z, core), slab: 4 (over y).
Axes of the slice: x: 4, y: 4, z: 4, core: 2. Of those that a mesh axis runs over, the one named last changes fastest.
Arguments:
- child_field: float32 [4, 1024, 2, 2048], P('slab', 'dir'), may hold values from -6 to 6
- child_src: int32 [4, 1024, 24], P('slab', 'dir'), may hold values from 0 to 1023
- child_type: int32 [4, 1024, 24], P('slab', 'dir'), may hold values from 0 to 159
- child_table: float32 [160, 2, 2048], replicated, may hold values from -2 to 2
- child_parent: int32 [4, 1024], P('slab', 'dir'), may hold values from 0 to 127
- child_octant: int32 [4, 1024], P('slab', 'dir'), may hold values from 0 to 7
- theta_interp: float32 [64, 32], replicated, may hold values from -1 to 1
- phi_interp: float32 [128, 64], replicated, may hold values from -0.75 to 0.75
- shift_table: float32 [8, 2, 8192], replicated, may hold values from -4 to 4
- readers: int32 [4, 2, 32], P('slab'), may hold values from 0 to 127
- parent_src: int32 [4, 128, 24], P('slab'), may hold values from 0 to 191
- parent_type: int32 [4, 128, 24], P('slab'), may hold values from 0 to 159
- parent_table: float32 [160, 2, 8192], P(None, None, 'dir'), may hold values from -2 to 2
Outputs:
- child_local: float32 [4, 1024, 2, 2048], P('slab', 'dir')
- parent_local: float32 [4, 128, 2, 8192], P('slab', None, None, 'dir')
Inputs may be any that keep to these rules, and one draw needn't show every extreme that they name: `child_src`: indices of child boxes of the same slab. `child_parent`: indices of parents of the same slab. `readers`: indices of parents of the sending slab.
All inputs are finite; a program needn't handle non-finite values.
Results may differ from a plain program's by a relative error of at most 0.00007.
Values sent between devices are 32-bit elements; how exact they have to be, the bound alone decides.
No kernel may reach another device: no remote copies, remote signals or barrier semaphores. Data moves between devices by JAX's collectives and lax.ppermute only.
A program may use at most 192 MiB of HBM per device.

v0:
```python
import functools

import jax
import jax.numpy as jnp
from jax import lax
from jax.experimental import pallas as pl
from jax.experimental.pallas import tpu as pltpu
from jax.sharding import PartitionSpec as P

F32 = jnp.float32
BF16 = jnp.bfloat16
I16 = jnp.int16
LANES = 128
HALF = 64
DIRS = 32
BOXES = 32
SLAB = DIRS * BOXES
ENTRIES = 24
TOGETHER = 4
GROUPS = ENTRIES // TOGETHER
AT_ONCE = 8
TYPES = 160
PARENTS = 128
BORDER = 32
OCTANTS = 8
LIST_ROWS = ENTRIES * BOXES // LANES
AT_TYPE = BOXES + LIST_ROWS
AT_OWNER = AT_TYPE + LIST_ROWS
SENT = 48

VMEM = pl.BlockSpec(memory_space=pltpu.VMEM)
SMEM = pl.BlockSpec(memory_space=pltpu.SMEM)
ANY = pl.BlockSpec(memory_space=pl.ANY)
HBM = pl.BlockSpec(memory_space=pltpu.HBM)
DMA = pltpu.SemaphoreType.DMA


def kept_out(*values):
    return tuple(pltpu.with_memory_space_constraint(value, pltpu.HBM) for value in values)


def shaped(*shape, dtype=F32):
    return jax.ShapeDtypeStruct(shape, dtype)


def call(kernel, out_shape, in_specs, out_specs, scratch, flops, nbytes, limit=24, **more):
    return pl.pallas_call(
        kernel,
        out_shape=out_shape,
        in_specs=in_specs,
        out_specs=out_specs,
        scratch_shapes=scratch,
        compiler_params=pltpu.CompilerParams(vmem_limit_bytes=limit << 20),
        cost_estimate=pl.CostEstimate(flops=flops, bytes_accessed=nbytes, transcendentals=0),
        **more,
    )


def lane_ids(rows):
    return lax.broadcasted_iota(jnp.int32, (rows, LANES), 1)


def swap_halves(value):
    return pltpu.roll(value, HALF, 1)


def split(value):
    high = value.astype(BF16)
    return high, (value - high.astype(F32)).astype(BF16)


def flat_rows(value):
    return jnp.concatenate([value[k : k + 1] for k in range(value.shape[0])], axis=1)


def one_hot(count, wanted):
    n = wanted.shape[1]
    tiled = jnp.concatenate([jnp.broadcast_to(wanted, (16, n)).astype(I16)] * (count // 16), axis=0)
    return jnp.where(lax.broadcasted_iota(I16, (count, n), 0) == tiled, BF16(1), BF16(0))


def pack_kernel(field, src, kind, parent, octant, out, held, lists, owned, packed, sems, out_sems):
    pieces = 4
    width = DIRS * HALF // pieces
    small = []
    for n, (ref, to) in enumerate(
        ((src, lists.at[0]), (kind, lists.at[1]), (parent, owned.at[0]), (octant, owned.at[1]))
    ):
        small.append(pltpu.make_async_copy(ref, to, sems.at[n]))
    large = []
    for n in range(pieces):
        cut = pl.ds(n * width, width)
        large.append(pltpu.make_async_copy(field.at[:, :, cut], held.at[:, :, cut], sems.at[4 + n]))
    for copy in small + large:
        copy.start()
    for copy in small:
        copy.wait()
    chunk = lane_ids(LIST_ROWS) // BOXES
    parts = []
    for n in range(2):
        rows = jnp.zeros((LIST_ROWS, LANES), F32)
        value = lists[n].astype(F32)
        value = jnp.concatenate([value] * 4, axis=1)
        for row in range(LIST_ROWS):
            for part in range(4):
                at = 4 * row + part
                here = (chunk == part) & (lax.broadcasted_iota(jnp.int32, (LIST_ROWS, LANES), 0) == row)
                rows = jnp.where(here, value[at : at + 1], rows)
        parts.append(rows)
    for n in range(2):
        parts.append(jnp.concatenate([owned[n].astype(F32)] * 4, axis=1))
    parts.append(jnp.zeros((SENT - AT_OWNER - 2, LANES), F32))
    tail = jnp.concatenate(parts, axis=0)
    low = lane_ids(BOXES) < HALF
    outs = []
    each = DIRS // pieces
    for n in range(pieces):
        for device in range(n * each, (n + 1) * each):
            packed[device, BOXES:SENT, :] = tail
        large[n].wait()
        for pair in range(n * each // 2, (n + 1) * each // 2):
            real = held[:, 0, pair * LANES : (pair + 1) * LANES]
            imag = held[:, 1, pair * LANES : (pair + 1) * LANES]
            packed[2 * pair, 0:BOXES, :] = jnp.where(low, real, swap_halves(imag))
            packed[2 * pair + 1, 0:BOXES, :] = jnp.where(low, swap_halves(real), imag)
        cut = pl.ds(n * each, each)
        outs.append(pltpu.make_async_copy(packed.at[cut], out.at[cut], out_sems.at[n]))
        outs[-1].start()
    for copy in outs:
        copy.wait()


def beside_kernel(
    me,
    packed,
    theta,
    child,
    kind,
    src,
    parent_table,
    out,
    child_out,
    weight_out,
    hot_out,
    held,
    table,
    sems,
):
    at = pl.multiple_of((me[0] // 2) * LANES, LANES)
    copies = [
        pltpu.make_async_copy(child.at[:, :, pl.ds(at, LANES)], held, sems.at[0]),
        pltpu.make_async_copy(parent_table, table, sems.at[1]),
    ]
    for copy in copies:
        copy.start()
    columns = [packed[pl.ds(c, DIRS, stride=SENT), :] for c in range(BOXES)]
    fields = jnp.concatenate(columns, axis=1)
    high, low = split(fields)
    theta_high, theta_low = split(theta[...])
    left = jnp.concatenate([theta_high, theta_high, theta_low], axis=1)
    right = jnp.concatenate([high, low, high], axis=0)
    finer = jnp.dot(left, right, preferred_element_type=F32)
    for c in range(BOXES):
        out[pl.ds(c, 2 * DIRS, stride=BOXES), :] = finer[:, c * LANES : (c + 1) * LANES]
    for copy in copies:
        copy.wait()
    pad = jnp.zeros((2 * LANES - TYPES, LANES), F32)
    odd = lax.rem(me[0], 2) == 1
    low = lane_ids(TYPES) < HALF
    real, imag = held[:, 0, :], held[:, 1, :]
    even_rows = jnp.where(low, real, swap_halves(imag))
    odd_rows = jnp.where(low, swap_halves(real), imag)
    rows = jnp.where(odd, odd_rows, even_rows)
    child_out[...] = jnp.transpose(jnp.concatenate([rows, pad], axis=0))
    weights = []
    for part in range(2):
        for polar in range(2):
            weight = jnp.concatenate([table[:, part, polar * LANES : (polar + 1) * LANES], pad], axis=0)
            weights.append(jnp.transpose(weight))
    weights = jnp.concatenate(split(jnp.concatenate(weights, axis=0)), axis=0)
    rows = 4 * LANES
    for n, at in enumerate(range(0, ENTRIES, TOGETHER)):
        hot_out[n] = one_hot(2 * LANES, flat_rows(src[at : at + TOGETHER, :]))
        hot = one_hot(2 * LANES, flat_rows(kind[at : at + TOGETHER, :]))
        value = jnp.dot(weights, hot, preferred_element_type=F32)
        weight_out[n] = value[:rows] + value[rows:]


def lookup(table, wanted):
    wanted = jnp.broadcast_to(wanted, (LANES, LANES))
    lanes = wanted & (LANES - 1)
    first = jnp.take_along_axis(table[:, :LANES], lanes, axis=1)
    second = jnp.take_along_axis(table[:, LANES:], lanes, axis=1)
    return jnp.where(wanted >= LANES, second, first)


def child_kernel(got, table, out, fields, src, kind):
    chunk = lane_ids(8) // BOXES
    for at, ref in ((BOXES, src), (AT_TYPE, kind)):
        for row in range(LIST_ROWS):
            rows = [got[pl.ds(i * SENT + at + row, 8, stride=4 * SENT), :] for i in range(4)]
            for part in range(4):
                value = jnp.zeros((8, LANES), F32)
                for i in range(4):
                    moved = rows[i] if i == part else pltpu.roll(rows[i], ((i - part) % 4) * BOXES, 1)
                    value = jnp.where(chunk == i, moved, value)
                ref[4 * row + part] = value.astype(jnp.int32)
    rows = jnp.concatenate([got[d * SENT : d * SENT + BOXES, :] for d in range(DIRS)], axis=0)
    fields[...] = jnp.concatenate(split(jnp.transpose(rows)), axis=0)
    tile = 2 * LANES

    def step(at, totals):
        real, imag = totals
        for n in range(AT_ONCE):
            entry = at * AT_ONCE + n
            wanted, kinds = flat_rows(src[entry]), kind[entry]
            picked = []
            for k in range(SLAB // tile):
                hot = one_hot(SLAB, wanted[:, k * tile : (k + 1) * tile])
                value = jnp.dot(fields[...], hot, preferred_element_type=F32)
                picked.append(value[:LANES] + value[LANES:])
            picked = jnp.concatenate(picked, axis=1)
            weight = jnp.concatenate([lookup(table, kinds[k : k + 1]) for k in range(8)], axis=1)
            fr, fi, wr, wi = picked[:HALF], picked[HALF:], weight[:HALF], weight[HALF:]
            real, imag = real + (wr * fr - wi * fi), imag + (wr * fi + wi * fr)
        return real, imag

    zero = jnp.zeros((HALF, SLAB), F32)
    real, imag = lax.fori_loop(0, ENTRIES // AT_ONCE, step, (zero, zero))
    out[...] = jnp.transpose(jnp.concatenate([real, imag], axis=0))


def unpack_kernel(got, out):
    low = lane_ids(BOXES) < HALF
    for pair in range(DIRS // 2):
        first, second = got[2 * pair], got[2 * pair + 1]
        out[:, 0, pair * LANES : (pair + 1) * LANES] = jnp.where(low, first, swap_halves(second))
        out[:, 1, pair * LANES : (pair + 1) * LANES] = jnp.where(low, swap_halves(first), second)


def field_kernel(me, got, owner, turn, shift_table, readers, out, up, down, shifts, sem):
    at = pl.multiple_of(me[0] * 2 * LANES, 2 * LANES)
    copy = pltpu.make_async_copy(shift_table.at[:, :, pl.ds(at, 2 * LANES)], shifts, sem)
    copy.start()
    chunk = lane_ids(8) // BOXES
    code = jnp.zeros((8, LANES), F32)
    for i in range(4):
        at = i * SENT + AT_OWNER
        parent = owner[pl.ds(at, 8, stride=4 * SENT), :]
        octant = owner[pl.ds(at + 1, 8, stride=4 * SENT), :]
        code = jnp.where(chunk == i, octant * PARENTS + parent, code)
    hot = one_hot(OCTANTS * PARENTS, flat_rows(code.astype(jnp.int32)))
    halves = []
    for polar in range(2):
        rows = [got[d, polar * BOXES : (polar + 1) * BOXES, :] for d in range(DIRS)]
        halves.extend(split(jnp.concatenate(rows, axis=0)))
    sums = jnp.dot(hot, jnp.concatenate(halves, axis=1), preferred_element_type=F32)
    none = jnp.zeros((HALF, LANES), F32)
    both = jnp.concatenate(
        [jnp.concatenate([turn[...], none], axis=1), jnp.concatenate([none, turn[...]], axis=1)], axis=0
    )
    both_high, both_low = split(both)
    right = jnp.concatenate([both_high, both_high, both_low], axis=0)
    copy.wait()
    columns = [None] * 4
    for polar in range(2):
        base = 2 * LANES * polar
        high, low = split(sums[:, base : base + LANES] + sums[:, base + LANES : base + 2 * LANES])
        fine = jnp.dot(jnp.concatenate([high, low, high], axis=1), right, preferred_element_type=F32)
        real = jnp.zeros((PARENTS, LANES), F32)
        imag = jnp.zeros((PARENTS, LANES), F32)
        for o in range(OCTANTS):
            fr = fine[o * PARENTS : (o + 1) * PARENTS, :LANES]
            fi = fine[o * PARENTS : (o + 1) * PARENTS, LANES:]
            sr = shifts[o, 0:1, polar * LANES : (polar + 1) * LANES]
            si = shifts[o, 1:2, polar * LANES : (polar + 1) * LANES]
            real += sr * fr - si * fi
            imag += sr * fi + si * fr
        columns[polar] = jnp.transpose(real)
        columns[2 + polar] = jnp.transpose(imag)
    field = jnp.concatenate(columns, axis=1)
    out[...] = field
    rows = lax.broadcasted_iota(jnp.int32, (4 * PARENTS, LANES), 0)
    lanes = lax.broadcasted_iota(jnp.int32, (4 * PARENTS, LANES), 1)
    picks = []
    for n in range(2):
        wanted = jnp.concatenate([readers[n : n + 1, :]] * 4, axis=1)
        hit = rows == (lanes // BORDER) * PARENTS + wanted
        picks.append(hit.astype(F32).astype(BF16))
    sent = jnp.dot(
        jnp.concatenate(split(field), axis=0), jnp.concatenate(picks, axis=1), preferred_element_type=F32
    )
    sent = sent[:LANES] + sent[LANES:]
    up[...] = sent[:, :LANES]
    down[...] = sent[:, LANES:]


def parent_kernel(own, lower, upper, weights, hots, out):
    lane = lane_ids(LANES)
    fields = []
    for m in range(4):
        below, above = lower[...], upper[...]
        if m > 0:
            below = pltpu.roll(below, (4 - m) * BORDER, 1)
        if m != 1:
            above = pltpu.roll(above, ((5 - m) % 4) * BORDER, 1)
        border = jnp.where(lane < BORDER, below, jnp.where(lane < 2 * BORDER, above, 0.0))
        fields.append(jnp.concatenate([own[:, m * PARENTS : (m + 1) * PARENTS], border], axis=1))
    fields = jnp.concatenate(split(jnp.concatenate(fields, axis=0)), axis=0)
    rows = 4 * LANES
    half = 2 * LANES
    real = jnp.zeros((half, PARENTS), F32)
    imag = jnp.zeros((half, PARENTS), F32)
    for group in range(GROUPS):
        picked = jnp.dot(fields, hots[group], preferred_element_type=F32)
        picked = picked[:rows] + picked[rows:]
        fr, fi, wr, wi = picked[:half], picked[half:], weights[group, :half], weights[group, half:]
        more_real = wr * fr - wi * fi
        more_imag = wr * fi + wi * fr
        for n in range(TOGETHER):
            real += more_real[:, n * PARENTS : (n + 1) * PARENTS]
            imag += more_imag[:, n * PARENTS : (n + 1) * PARENTS]
    out[:, 0, :] = jnp.transpose(real)
    out[:, 1, :] = jnp.transpose(imag)


def on_device(
    child_field,
    child_src,
    child_type,
    child_table,
    child_parent,
    child_octant,
    theta_interp,
    phi_interp,
    shift_table,
    readers,
    parent_src,
    parent_type,
    parent_table,
):
    me = lax.axis_index("dir").astype(jnp.int32)[None]

    packed = call(
        pack_kernel,
        shaped(DIRS, SENT, LANES),
        [HBM] * 5,
        HBM,
        [
            pltpu.VMEM((BOXES, 2, DIRS * HALF), F32),
            pltpu.VMEM((2, ENTRIES, BOXES), jnp.int32),
            pltpu.VMEM((2, 1, BOXES), jnp.int32),
            pltpu.VMEM((DIRS, SENT, LANES), F32),
            DMA((8,)),
            DMA((4,)),
        ],
        1 << 20,
        3 << 20,
    )(
        *kept_out(
            child_field[0],
            jnp.swapaxes(child_src[0], 0, 1),
            jnp.swapaxes(child_type[0], 0, 1),
            child_parent,
            child_octant,
        )
    )
    got = lax.all_to_all(packed, "dir", split_axis=0, concat_axis=0)
    got = got.reshape(DIRS * SENT, LANES)

    finer, child_rows, parent_weights, parent_hot = call(
        beside_kernel,
        (
            shaped(2 * DIRS * BOXES, LANES),
            shaped(LANES, 2 * LANES),
            pltpu.VMEM((GROUPS, 4 * LANES, TOGETHER * PARENTS), F32),
            pltpu.VMEM((GROUPS, 2 * LANES, TOGETHER * PARENTS), BF16),
        ),
        [SMEM, VMEM, VMEM, HBM, VMEM, VMEM, HBM],
        (VMEM,) * 4,
        [pltpu.VMEM((TYPES, 2, LANES), F32), pltpu.VMEM((TYPES, 2, 2 * LANES), F32), DMA((2,))],
        1 << 30,
        4 << 20,
        limit=32,
    )(
        me,
        packed.reshape(DIRS * SENT, LANES),
        theta_interp,
        *kept_out(child_table),
        jnp.swapaxes(parent_type[0], 0, 1),
        jnp.swapaxes(parent_src[0], 0, 1),
        *kept_out(parent_table),
    )
    finer_got = lax.all_to_all(finer.reshape(DIRS, 2 * BOXES, LANES), "dir", split_axis=0, concat_axis=0)

    child_rows_out = call(
        child_kernel,
        shaped(SLAB, LANES),
        [VMEM] * 2,
        VMEM,
        [
            pltpu.VMEM((2 * LANES, SLAB), BF16),
            pltpu.VMEM((ENTRIES, 8, LANES), jnp.int32),
            pltpu.VMEM((ENTRIES, 8, LANES), jnp.int32),
        ],
        16 << 30,
        4 << 20,
    )(got, child_rows)
    child_back = lax.all_to_all(child_rows_out.reshape(DIRS, BOXES, LANES), "dir", split_axis=0, concat_axis=0)

    own, to_upper, to_lower = call(
        field_kernel,
        (shaped(LANES, 4 * PARENTS), shaped(LANES, LANES), shaped(LANES, LANES)),
        [SMEM, VMEM, VMEM, VMEM, HBM, VMEM],
        (VMEM,) * 3,
        [pltpu.VMEM((OCTANTS, 2, 2 * LANES), F32), DMA],
        2 << 30,
        4 << 20,
    )(me, finer_got, got, jnp.swapaxes(phi_interp, 0, 1), *kept_out(shift_table), readers[0])
    slabs = lax.axis_size("slab")
    from_lower = lax.ppermute(to_upper, "slab", [(s, s + 1) for s in range(slabs - 1)])
    from_upper = lax.ppermute(to_lower, "slab", [(s + 1, s) for s in range(slabs - 1)])

    child_out = call(
        unpack_kernel, shaped(BOXES, 2, DIRS * HALF), [VMEM], VMEM, [], 1 << 20, 2 << 20
    )(child_back)

    parent_out = call(
        parent_kernel,
        shaped(PARENTS, 2, 2 * LANES),
        [VMEM] * 5,
        VMEM,
        [],
        4 << 30,
        8 << 20,
    )(own, from_lower, from_upper, parent_weights, parent_hot)
    return (child_out[None], parent_out[None])


def solution(mesh):
    return jax.shard_map(
        on_device,
        mesh=mesh,
        in_specs=(
            P("slab", "dir", None, None),
            P("slab", "dir", None),
            P("slab", "dir", None),
            P(),
            P("slab", "dir"),
            P("slab", "dir"),
            P(),
            P(),
            P(),
            P("slab", None, None),
            P("slab", None, None),
            P("slab", None, None),
            P(None, None, "dir"),
        ),
        out_specs=(P("slab", "dir", None, None), P("slab", None, None, "dir")),
        check_vma=False,
    )
```

profile of v0, /device:TPU:2, one launch (start us, length us, event | category | flops | bytes accessed | tf_op | source)
XLA Modules:
  0.0 70.9 jit_solution(8440715910719630097)
XLA Ops:
  0.6 0.0 copy-start.8
  0.6 0.0 copy-start.1
  0.7 0.0 copy-start.2
  0.7 2.5 %shard_map.140 = f32[32,48,128]{2,1,0:T(8,128)} custom-call(f32[32,2,2048]{2,1,0:T(2,128)} %bitcast.28, s32[24,32]{1,0:T(8,128)} %bitcast.30, s32[24,32]{1,0:T(8,128)} %bitcast.31, s32[1,32]{1,0:T(1,128)} %parent.1, s32[1,32]{1,0:T(1,128)} %octant.1), custom_call_target="tpu_custom_call" | custom-call | flops 1048576 | bytes 3145728 | tf_op jit(solution)/shard_map/pallas_call | solution.py:344
  3.2 8.5 %all-to-all-start = ((f32[32,48,128]{2,1,0:T(8,128)}), f32[32,48,128]{2,1,0:T(8,128)S(1)}, u32[]{:S(2)}, u32[]{:S(2)}) async-start(f32[32,48,128]{2,1,0:T(8,128)} %shard_map.140), calls=%async_computation | async-start | bytes 1572864 | tf_op jit(solution)/shard_map/all_to_all | solution.py:368
  11.7 0.1 copy.15.theta
  11.8 4.4 %shard_map.141 = (f32[2048,128]{1,0:T(8,128)}, f32[128,256]{1,0:T(8,128)S(1)}, f32[6,512,512]{2,1,0:T(8,128)S(1)}, bf16[6,256,512]{2,1,0:T(8,128)(2,1)S(1)}) custom-call(s32[1]{0:T(128)} %bitcast.6.me, f32[1536,128]{1,0:T(8,128)} %bitcast.7.packed, f32[64,32]{1,0:T(8,128)S(1)} %copy.15.theta, f32[160,2,2048]{2,1,0:T(2,128)} %child.1, ...), custom_call_target="tpu_custom_call" | custom-call | flops 1073741824 | bytes 4194304 | tf_op jit(solution)/shard_map/pallas_call | solution.py:371
  16.2 2.6 %copy-done.4 = f32[6,512,512]{2,1,0:T(8,128)} copy-done((f32[6,512,512]{2,1,0:T(8,128)}, f32[6,512,512]{2,1,0:T(8,128)S(1)}, u32[]{:S(2)}) %copy-start.4) | copy-done | bytes 6291480
  18.9 1.2 %copy-done.6 = bf16[6,256,512]{2,1,0:T(8,128)(2,1)} copy-done((bf16[6,256,512]{2,1,0:T(8,128)(2,1)}, bf16[6,256,512]{2,1,0:T(8,128)(2,1)S(1)}, u32[]{:S(2)}) %copy-start.6) | copy-done | bytes 1572888
  20.1 3.7 %all-to-all-done = f32[32,48,128]{2,1,0:T(8,128)S(1)} async-done(((f32[32,48,128]{2,1,0:T(8,128)}), f32[32,48,128]{2,1,0:T(8,128)S(1)}, u32[]{:S(2)}, u32[]{:S(2)}) %all-to-all-start) | async-done | bytes 786464 | tf_op jit(solution)/shard_map/all_to_all | solution.py:368
  23.7 6.0 %all-to-all-start.2 = ((f32[32,64,128]{2,1,0:T(8,128)}), f32[32,64,128]{2,1,0:T(8,128)S(1)}, u32[]{:S(2)}, u32[]{:S(2)}) async-start(f32[32,64,128]{2,1,0:T(8,128)} %bitcast.14), calls=%async_computation.2 | async-start | bytes 2097152 | tf_op jit(solution)/shard_map/all_to_all | solution.py:394
  29.7 0.0 copy-start
  29.8 0.0 copy-start.3
  29.8 15.9 %shard_map.142 = f32[1024,128]{1,0:T(8,128)} custom-call(f32[1536,128]{1,0:T(8,128)S(1)} %bitcast.22, f32[128,256]{1,0:T(8,128)S(1)} %get-tuple-element.9.table), custom_call_target="tpu_custom_call" | custom-call | flops 17179869184 | bytes 4194304 | tf_op jit(solution)/shard_map/pallas_call | solution.py:396
  45.7 0.0 all-to-all-done.2.got
  45.7 7.4 %all-to-all-start.1 = ((f32[32,32,128]{2,1,0:T(8,128)}), f32[32,32,128]{2,1,0:T(8,128)S(1)}, u32[]{:S(2)}, u32[]{:S(2)}) async-start(f32[32,32,128]{2,1,0:T(8,128)} %bitcast.12), calls=%async_computation.1 | async-start | bytes 1048576 | tf_op jit(solution)/shard_map/all_to_all | solution.py:409
  53.1 3.6 %shard_map.144 = (f32[128,512]{1,0:T(8,128)S(1)}, f32[128,128]{1,0:T(8,128)S(1)}, f32[128,128]{1,0:T(8,128)S(1)}) custom-call(s32[1]{0:T(128)} %bitcast.6.me, f32[32,64,128]{2,1,0:T(8,128)S(1)} %all-to-all-done.2.got, f32[1536,128]{1,0:T(8,128)S(1)} %bitcast.23, f32[64,128]{1,0:T(8,128)S(1)} %bitcast.24, f32[8,2,8192]{2,1,0:T(2,128)} %shift_table.1, ...), custom_call_target="tpu_custom_call" | custom-call | flops 2147483648 | bytes 4194304 | tf_op jit(solution)/shard_map/pallas_call | solution.py:411
  56.7 3.5 %collective-permute-start = (f32[128,128]{1,0:T(8,128)S(1)}, f32[128,128]{1,0:T(8,128)S(1)}, u32[]{:S(2)}, u32[]{:S(2)}) collective-permute-start(f32[128,128]{1,0:T(8,128)S(1)} %get-tuple-element.12), channel_id=1, source_target_pairs={{0,1},{1,2},{2,3},{4,5},{5,6},{6,7},{8,9},{9,10},{10,11},{12,13},{... | collective-permute-start | bytes 196616 | tf_op jit(solution)/shard_map/ppermute | solution.py:421
  60.2 1.3 %collective-permute-start.1 = (f32[128,128]{1,0:T(8,128)S(1)}, f32[128,128]{1,0:T(8,128)S(1)}, u32[]{:S(2)}, u32[]{:S(2)}) collective-permute-start(f32[128,128]{1,0:T(8,128)S(1)} %get-tuple-element.13), channel_id=1, source_target_pairs={{1,0},{2,1},{3,2},{5,4},{6,5},{7,6},{9,8},{10,9},{11,10},{13,12},{... | collective-permute-start | bytes 196616 | tf_op jit(solution)/shard_map/ppermute | solution.py:422
  61.5 0.6 collective-permute-done.lower
  62.1 4.3 %collective-permute-done.1.upper = f32[128,128]{1,0:T(8,128)S(1)} collective-permute-done((f32[128,128]{1,0:T(8,128)S(1)}, f32[128,128]{1,0:T(8,128)S(1)}, u32[]{:S(2)}, u32[]{:S(2)}) %collective-permute-start.1) | collective-permute-done | bytes 65568 | tf_op jit(solution)/shard_map/ppermute | solution.py:422
  66.4 3.2 %shard_map.145 = f32[128,2,256]{2,1,0:T(2,128)} custom-call(f32[128,512]{1,0:T(8,128)S(1)} %get-tuple-element.11.own, f32[128,128]{1,0:T(8,128)S(1)} %collective-permute-done.lower, f32[128,128]{1,0:T(8,128)S(1)} %collective-permute-done.1.upper, f32[6,512,512]{2,1,0:T(8,128)S(1)} %copy-done.5, bf16[6,256,512]{2,1,0:T(8,128)(2,1)S(1)} %copy-done.7), custom_call_target="tpu_custom_call" | custom-call | flops 4294967296 | bytes 8388608 | tf_op jit(solution)/shard_map/pallas_call | solution.py:428
  69.5 0.0 all-to-all-done.1.got
  69.5 1.4 %shard_map.143 = f32[32,2,2048]{2,1,0:T(2,128)} custom-call(f32[32,32,128]{2,1,0:T(8,128)S(1)} %all-to-all-done.1.got), custom_call_target="tpu_custom_call" | custom-call | flops 1048576 | bytes 2097152 | tf_op jit(solution)/shard_map/pallas_call | solution.py:424
  (11 shorter events, 0.0 us)
Async XLA Ops:
  0.6 11.1 %copy-start.8 = (f32[64,32]{0,1:T(8,128)S(1)}, f32[64,32]{0,1:T(8,128)}, u32[]{:S(2)}) copy-start(f32[64,32]{0,1:T(8,128)} %param.19) | copy-start | bytes 24580
  0.6 11.1 %copy-start.1 = (s32[1,128,24]{1,2,0:T(8,128)S(1)}, s32[1,128,24]{1,2,0:T(8,128)}, u32[]{:S(2)}) copy-start(s32[1,128,24]{1,2,0:T(8,128)} %param.24) | copy-start | bytes 36868
  0.7 11.1 %copy-start.2 = (s32[1,128,24]{1,2,0:T(8,128)S(1)}, s32[1,128,24]{1,2,0:T(8,128)}, u32[]{:S(2)}) copy-start(s32[1,128,24]{1,2,0:T(8,128)} %param.23) | copy-start | bytes 36868
  3.2 20.5 %all-to-all-start = ((f32[32,48,128]{2,1,0:T(8,128)}), f32[32,48,128]{2,1,0:T(8,128)S(1)}, u32[]{:S(2)}, u32[]{:S(2)}) async-start(f32[32,48,128]{2,1,0:T(8,128)} %shard_map.140), calls=%async_computation | async-start | bytes 1572864 | tf_op jit(solution)/shard_map/all_to_all | solution.py:368
  16.2 2.7 %copy-start.4 = (f32[6,512,512]{2,1,0:T(8,128)}, f32[6,512,512]{2,1,0:T(8,128)S(1)}, u32[]{:S(2)}) copy-start(f32[6,512,512]{2,1,0:T(8,128)S(1)} %get-tuple-element.14.weights) | copy-start | bytes 18874372
  18.9 1.2 %copy-start.6 = (bf16[6,256,512]{2,1,0:T(8,128)(2,1)}, bf16[6,256,512]{2,1,0:T(8,128)(2,1)S(1)}, u32[]{:S(2)}) copy-start(bf16[6,256,512]{2,1,0:T(8,128)(2,1)S(1)} %get-tuple-element.15.hots) | copy-start | bytes 4718596
  23.7 22.0 %all-to-all-start.2 = ((f32[32,64,128]{2,1,0:T(8,128)}), f32[32,64,128]{2,1,0:T(8,128)S(1)}, u32[]{:S(2)}, u32[]{:S(2)}) async-start(f32[32,64,128]{2,1,0:T(8,128)} %bitcast.14), calls=%async_computation.2 | async-start | bytes 2097152 | tf_op jit(solution)/shard_map/all_to_all | solution.py:394
  29.7 23.3 %copy-start = (f32[128,64]{0,1:T(8,128)S(1)}, f32[128,64]{0,1:T(8,128)}, u32[]{:S(2)}) copy-start(f32[128,64]{0,1:T(8,128)} %param.20) | copy-start | bytes 98308
  29.8 23.3 %copy-start.3 = (s32[1,2,32]{2,1,0:T(2,128)S(1)}, s32[1,2,32]{2,1,0:T(2,128)}, u32[]{:S(2)}) copy-start(s32[1,2,32]{2,1,0:T(2,128)} %param.22) | copy-start | bytes 772
  45.7 23.8 %all-to-all-start.1 = ((f32[32,32,128]{2,1,0:T(8,128)}), f32[32,32,128]{2,1,0:T(8,128)S(1)}, u32[]{:S(2)}, u32[]{:S(2)}) async-start(f32[32,32,128]{2,1,0:T(8,128)} %bitcast.12), calls=%async_computation.1 | async-start | bytes 1048576 | tf_op jit(solution)/shard_map/all_to_all | solution.py:409
  53.1 13.3 %copy-start.5 = (f32[6,512,512]{2,1,0:T(8,128)S(1)}, f32[6,512,512]{2,1,0:T(8,128)}, u32[]{:S(2)}) copy-start(f32[6,512,512]{2,1,0:T(8,128)} %copy-done.4) | copy-start | bytes 18874372
  53.1 13.2 %copy-start.7 = (bf16[6,256,512]{2,1,0:T(8,128)(2,1)S(1)}, bf16[6,256,512]{2,1,0:T(8,128)(2,1)}, u32[]{:S(2)}) copy-start(bf16[6,256,512]{2,1,0:T(8,128)(2,1)} %copy-done.6) | copy-start | bytes 4718596
  56.7 5.4 %collective-permute-start = (f32[128,128]{1,0:T(8,128)S(1)}, f32[128,128]{1,0:T(8,128)S(1)}, u32[]{:S(2)}, u32[]{:S(2)}) collective-permute-start(f32[128,128]{1,0:T(8,128)S(1)} %get-tuple-element.12), channel_id=1, source_target_pairs={{0,1},{1,2},{2,3},{4,5},{5,6},{6,7},{8,9},{9,10},{10,11},{12,13},{... | collective-permute-start | bytes 196616 | tf_op jit(solution)/shard_map/ppermute | solution.py:421
  60.2 6.2 %collective-permute-start.1 = (f32[128,128]{1,0:T(8,128)S(1)}, f32[128,128]{1,0:T(8,128)S(1)}, u32[]{:S(2)}, u32[]{:S(2)}) collective-permute-start(f32[128,128]{1,0:T(8,128)S(1)} %get-tuple-element.13), channel_id=1, source_target_pairs={{1,0},{2,1},{3,2},{5,4},{6,5},{7,6},{9,8},{10,9},{11,10},{13,12},{... | collective-permute-start | bytes 196616 | tf_op jit(solution)/shard_map/ppermute | solution.py:422
where the time goes:
time: 71.4 us; the launch traced here: 70.9 us
  Pallas kernels  31 us (43%)
  starting transfers between devices  26.7 us (37%)
  waiting for transfers between devices  8.52 us (12%)
  local copies, waits for them, and re-layouts  3.92 us (5%)
  between operations  0.8 us (1%)
    pallas_call x1, Pallas kernels, on_device(): call(child_kernel, shaped(SLAB, LANES), [VMEM] * 2, VMEM, [pltpu.VMEM((2...  15.9 us
    all_to_all x1, starting transfers between devices, on_device(): got = lax.all_to_all(packed, 'dir', split_axis=0, concat_axis=0)  8.48 us
    all_to_all x1, starting transfers between devices, on_device(): lax.all_to_all(child_rows_out.reshape(DIRS, BOXES, LANES), 'dir', split_a...  7.38 us
    all_to_all x1, starting transfers between devices, on_device(): lax.all_to_all(finer.reshape(DIRS, 2 * BOXES, LANES), 'dir', split_axis=0...  6.03 us
    pallas_call x1, Pallas kernels, on_device(): call(beside_kernel, (shaped(2 * DIRS * BOXES, LANES), shaped(LANES, 2 * L...  4.44 us
    ppermute x1, waiting for transfers between devices, on_device(): lax.ppermute(to_lower, 'slab', [(s + 1, s) for s in range(slabs - 1)])  4.27 us
    unnamed x19, local copies, waits for them, and re-layouts  3.92 us
    all_to_all x1, waiting for transfers between devices, on_device(): got = lax.all_to_all(packed, 'dir', split_axis=0, concat_axis=0)  3.65 us
  transfers between devices with their start and end apart: 5, of which 3 were waited for; matrix products, arithmetic and copies ran while one was open for 0% of the time, Pallas kernels for 38%

commit v1 on v0

--- a/solution.py
+++ b/solution.py
@@ -194,7 +194,21 @@
     return jnp.where(wanted >= LANES, second, first)
 
 
-def child_kernel(got, table, out, fields, src, kind):
+def pick(exact, wanted):
+    wanted = jnp.broadcast_to(wanted, (LANES, LANES))
+    lanes = wanted & (LANES - 1)
+    values = [
+        jnp.take_along_axis(exact[:, k * LANES : (k + 1) * LANES], lanes, axis=1) for k in range(SLAB // LANES)
+    ]
+    bit = LANES
+    while len(values) > 1:
+        upper = (wanted & bit) != 0
+        values = [jnp.where(upper, values[n + 1], values[n]) for n in range(0, len(values), 2)]
+        bit *= 2
+    return values[0]
+
+
+def child_kernel(got, table, out, fields, exact, src, kind, held, sems):
     chunk = lane_ids(8) // BOXES
     for at, ref in ((BOXES, src), (AT_TYPE, kind)):
         for row in range(LIST_ROWS):
@@ -206,16 +220,20 @@
                     value = jnp.where(chunk == i, moved, value)
                 ref[4 * row + part] = value.astype(jnp.int32)
     rows = jnp.concatenate([got[d * SENT : d * SENT + BOXES, :] for d in range(DIRS)], axis=0)
-    fields[...] = jnp.concatenate(split(jnp.transpose(rows)), axis=0)
+    exact[...] = jnp.transpose(rows)
+    fields[...] = jnp.concatenate(split(exact[...]), axis=0)
     tile = 2 * LANES
 
-    def step(at, totals):
+    def step(step_at, totals):
         real, imag = totals
         for n in range(AT_ONCE):
-            entry = at * AT_ONCE + n
+            entry = step_at * AT_ONCE + n
             wanted, kinds = flat_rows(src[entry]), kind[entry]
             picked = []
             for k in range(SLAB // tile):
+                if n % 2 == 1 and k == SLAB // tile - 1:
+                    picked.extend(pick(exact, wanted[:, at : at + LANES]) for at in (k * tile, k * tile + LANES))
+                    continue
                 hot = one_hot(SLAB, wanted[:, k * tile : (k + 1) * tile])
                 value = jnp.dot(fields[...], hot, preferred_element_type=F32)
                 picked.append(value[:LANES] + value[LANES:])
@@ -227,21 +245,35 @@
 
     zero = jnp.zeros((HALF, SLAB), F32)
     real, imag = lax.fori_loop(0, ENTRIES // AT_ONCE, step, (zero, zero))
-    out[...] = jnp.transpose(jnp.concatenate([real, imag], axis=0))
-
-
-def unpack_kernel(got, out):
+    total = jnp.concatenate([real, imag], axis=0)
+    copies = []
+    for n in range(4):
+        cut = pl.ds(n * tile, tile)
+        held[cut, :] = jnp.transpose(total[:, n * tile : (n + 1) * tile])
+        copies.append(pltpu.make_async_copy(held.at[cut], out.at[cut], sems.at[n]))
+        copies[-1].start()
+    for copy in copies:
+        copy.wait()
+
+
+def unpack_kernel(got, out, held, sems):
     low = lane_ids(BOXES) < HALF
-    for pair in range(DIRS // 2):
-        first, second = got[2 * pair], got[2 * pair + 1]
-        out[:, 0, pair * LANES : (pair + 1) * LANES] = jnp.where(low, first, swap_halves(second))
-        out[:, 1, pair * LANES : (pair + 1) * LANES] = jnp.where(low, swap_halves(first), second)
-
-
-def field_kernel(me, got, owner, turn, shift_table, readers, out, up, down, shifts, sem):
-    at = pl.multiple_of(me[0] * 2 * LANES, 2 * LANES)
-    copy = pltpu.make_async_copy(shift_table.at[:, :, pl.ds(at, 2 * LANES)], shifts, sem)
-    copy.start()
+    pieces = 4
+    pairs = DIRS // 2 // pieces
+    copies = []
+    for n in range(pieces):
+        for pair in range(n * pairs, (n + 1) * pairs):
+            first, second = got[2 * pair], got[2 * pair + 1]
+            held[:, 0, pair * LANES : (pair + 1) * LANES] = jnp.where(low, first, swap_halves(second))
+            held[:, 1, pair * LANES : (pair + 1) * LANES] = jnp.where(low, swap_halves(first), second)
+        cut = pl.ds(n * pairs * LANES, pairs * LANES)
+        copies.append(pltpu.make_async_copy(held.at[:, :, cut], out.at[:, :, cut], sems.at[n]))
+        copies[-1].start()
+    for copy in copies:
+        copy.wait()
+
+
+def family(owner):
     chunk = lane_ids(8) // BOXES
     code = jnp.zeros((8, LANES), F32)
     for i in range(4):
@@ -249,7 +281,10 @@
         parent = owner[pl.ds(at, 8, stride=4 * SENT), :]
         octant = owner[pl.ds(at + 1, 8, stride=4 * SENT), :]
         code = jnp.where(chunk == i, octant * PARENTS + parent, code)
-    hot = one_hot(OCTANTS * PARENTS, flat_rows(code.astype(jnp.int32)))
+    return flat_rows(code.astype(jnp.int32))
+
+
+def shifted_sums(hot, got, turn, shifts, count):
     halves = []
     for polar in range(2):
         rows = [got[d, polar * BOXES : (polar + 1) * BOXES, :] for d in range(DIRS)]
@@ -261,51 +296,69 @@
     )
     both_high, both_low = split(both)
     right = jnp.concatenate([both_high, both_high, both_low], axis=0)
-    copy.wait()
-    columns = [None] * 4
+    results = []
     for polar in range(2):
         base = 2 * LANES * polar
         high, low = split(sums[:, base : base + LANES] + sums[:, base + LANES : base + 2 * LANES])
         fine = jnp.dot(jnp.concatenate([high, low, high], axis=1), right, preferred_element_type=F32)
-        real = jnp.zeros((PARENTS, LANES), F32)
-        imag = jnp.zeros((PARENTS, LANES), F32)
+        real = jnp.zeros((count, LANES), F32)
+        imag = jnp.zeros((count, LANES), F32)
         for o in range(OCTANTS):
-            fr = fine[o * PARENTS : (o + 1) * PARENTS, :LANES]
-            fi = fine[o * PARENTS : (o + 1) * PARENTS, LANES:]
+            fr = fine[o * count : (o + 1) * count, :LANES]
+            fi = fine[o * count : (o + 1) * count, LANES:]
             sr = shifts[o, 0:1, polar * LANES : (polar + 1) * LANES]
             si = shifts[o, 1:2, polar * LANES : (polar + 1) * LANES]
             real += sr * fr - si * fi
             imag += sr * fi + si * fr
-        columns[polar] = jnp.transpose(real)
-        columns[2 + polar] = jnp.transpose(imag)
-    field = jnp.concatenate(columns, axis=1)
-    out[...] = field
-    rows = lax.broadcasted_iota(jnp.int32, (4 * PARENTS, LANES), 0)
-    lanes = lax.broadcasted_iota(jnp.int32, (4 * PARENTS, LANES), 1)
-    picks = []
-    for n in range(2):
-        wanted = jnp.concatenate([readers[n : n + 1, :]] * 4, axis=1)
-        hit = rows == (lanes // BORDER) * PARENTS + wanted
-        picks.append(hit.astype(F32).astype(BF16))
-    sent = jnp.dot(
-        jnp.concatenate(split(field), axis=0), jnp.concatenate(picks, axis=1), preferred_element_type=F32
-    )
-    sent = sent[:LANES] + sent[LANES:]
-    up[...] = sent[:, :LANES]
-    down[...] = sent[:, LANES:]
+        results.append((real, imag))
+    return results
+
+
+def shift_copy(me, shift_table, shifts, sem):
+    at = pl.multiple_of(me[0] * 2 * LANES, 2 * LANES)
+    return pltpu.make_async_copy(shift_table.at[:, :, pl.ds(at, 2 * LANES)], shifts, sem)
+
+
+def border_kernel(me, got, owner, turn, shift_table, readers, up, down, shifts, sem):
+    copy = shift_copy(me, shift_table, shifts, sem)
+    copy.start()
+    count = 2 * BORDER
+    wanted = jnp.concatenate([readers[0:1, :], readers[1:2, :]], axis=1).astype(F32)
+    wanted = jnp.concatenate([wanted, jnp.zeros((1, LANES - count), F32)], axis=1)
+    wanted = jnp.transpose(jnp.broadcast_to(wanted, (LANES, LANES)))[:count].astype(jnp.int32)
+    code = family(owner)
+    blocks = []
+    for k in range(SLAB // LANES):
+        block = jnp.broadcast_to(code[:, k * LANES : (k + 1) * LANES], (count, LANES)).astype(I16)
+        hits = []
+        for o in range(OCTANTS):
+            here = (wanted + o * PARENTS).astype(I16)
+            hits.append(jnp.where(here == block, BF16(1), BF16(0)))
+        blocks.append(jnp.concatenate(hits, axis=0))
+    hot = jnp.concatenate(blocks, axis=1)
+    copy.wait()
+    (real0, imag0), (real1, imag1) = shifted_sums(hot, got, turn, shifts, count)
+    for m, value in enumerate((real0, real1, imag0, imag1)):
+        up[:, m * LANES : (m + 1) * LANES] = value[:BORDER]
+        down[:, m * LANES : (m + 1) * LANES] = value[BORDER:]
+
+
+def own_kernel(me, got, owner, turn, shift_table, out, shifts, sem):
+    copy = shift_copy(me, shift_table, shifts, sem)
+    copy.start()
+    hot = one_hot(OCTANTS * PARENTS, family(owner))
+    copy.wait()
+    (real0, imag0), (real1, imag1) = shifted_sums(hot, got, turn, shifts, PARENTS)
+    for m, value in enumerate((real0, real1, imag0, imag1)):
+        out[:, m * PARENTS : (m + 1) * PARENTS] = jnp.transpose(value)
 
 
 def parent_kernel(own, lower, upper, weights, hots, out):
-    lane = lane_ids(LANES)
+    border = jnp.concatenate([lower[...], upper[...], jnp.zeros((2 * BORDER, 4 * LANES), F32)], axis=0)
     fields = []
     for m in range(4):
-        below, above = lower[...], upper[...]
-        if m > 0:
-            below = pltpu.roll(below, (4 - m) * BORDER, 1)
-        if m != 1:
-            above = pltpu.roll(above, ((5 - m) % 4) * BORDER, 1)
-        border = jnp.where(lane < BORDER, below, jnp.where(lane < 2 * BORDER, above, 0.0))
-        fields.append(jnp.concatenate([own[:, m * PARENTS : (m + 1) * PARENTS], border], axis=1))
+        turned = jnp.transpose(border[:, m * LANES : (m + 1) * LANES])
+        fields.append(jnp.concatenate([own[:, m * PARENTS : (m + 1) * PARENTS], turned], axis=1))
     fields = jnp.concatenate(split(jnp.concatenate(fields, axis=0)), axis=0)
     rows = 4 * LANES
     half = 2 * LANES
@@ -397,32 +450,52 @@
         child_kernel,
         shaped(SLAB, LANES),
         [VMEM] * 2,
-        VMEM,
+        HBM,
         [
             pltpu.VMEM((2 * LANES, SLAB), BF16),
+            pltpu.VMEM((LANES, SLAB), F32),
             pltpu.VMEM((ENTRIES, 8, LANES), jnp.int32),
             pltpu.VMEM((ENTRIES, 8, LANES), jnp.int32),
+            pltpu.VMEM((SLAB, LANES), F32),
+            DMA((4,)),
         ],
         16 << 30,
         4 << 20,
     )(got, child_rows)
     child_back = lax.all_to_all(child_rows_out.reshape(DIRS, BOXES, LANES), "dir", split_axis=0, concat_axis=0)
 
-    own, to_upper, to_lower = call(
-        field_kernel,
-        (shaped(LANES, 4 * PARENTS), shaped(LANES, LANES), shaped(LANES, LANES)),
+    turn = jnp.swapaxes(phi_interp, 0, 1)
+    (shift_rows,) = kept_out(shift_table)
+    to_upper, to_lower = call(
+        border_kernel,
+        (shaped(BORDER, 4 * LANES),) * 2,
         [SMEM, VMEM, VMEM, VMEM, HBM, VMEM],
-        (VMEM,) * 3,
+        (VMEM,) * 2,
+        [pltpu.VMEM((OCTANTS, 2, 2 * LANES), F32), DMA],
+        1 << 30,
+        4 << 20,
+    )(me, finer_got, got, turn, shift_rows, readers[0])
+    own = call(
+        own_kernel,
+        pltpu.VMEM((LANES, 4 * PARENTS), F32),
+        [SMEM, VMEM, VMEM, VMEM, HBM],
+        VMEM,
         [pltpu.VMEM((OCTANTS, 2, 2 * LANES), F32), DMA],
         2 << 30,
         4 << 20,
-    )(me, finer_got, got, jnp.swapaxes(phi_interp, 0, 1), *kept_out(shift_table), readers[0])
+    )(me, finer_got, got, turn, shift_rows)
     slabs = lax.axis_size("slab")
     from_lower = lax.ppermute(to_upper, "slab", [(s, s + 1) for s in range(slabs - 1)])
     from_upper = lax.ppermute(to_lower, "slab", [(s + 1, s) for s in range(slabs - 1)])
 
     child_out = call(
-        unpack_kernel, shaped(BOXES, 2, DIRS * HALF), [VMEM], VMEM, [], 1 << 20, 2 << 20
+        unpack_kernel,
+        shaped(BOXES, 2, DIRS * HALF),
+        [VMEM],
+        HBM,
+        [pltpu.VMEM((BOXES, 2, DIRS * HALF), F32), DMA((4,))],
+        1 << 20,
+        2 << 20,
     )(child_back)
 
     parent_out = call(

time: 71.4 us -> 69.7 us (0.976)
  waiting for transfers between devices: 8.52 us -> 5.66 us
    ppermute x1, waiting for transfers between devices: 4.27 us -> 2 us  [on_device(): lax.ppermute(to_lower, 'slab', [(s + 1, s) for s in range(slabs - 1)])]
    pallas_call x3 -> x4, Pallas kernels: 20.8 us -> 21.3 us  [the longest x1 15.5 us: on_device(): call(child_kernel, shaped(SLAB, LANES), [VMEM] * 2, HBM, [pltpu.VMEM((2 *...]
    unnamed x19 -> x21, local copies, waits for them, and re-layouts: 3.92 us -> 3.92 us
  transfers between devices with their start and end apart: 5 -> 5, of which waited for: 3 -> 2; matrix products, arithmetic and copies ran while one was open for 0% -> 0% of each run, Pallas kernels for 38% -> 40%
where the time goes in v1:
time: 69.7 us; the launch traced here: 69.2 us
  Pallas kernels  31.5 us (45%)
  starting transfers between devices  27.1 us (39%)
  waiting for transfers between devices  5.66 us (8%)
  local copies, waits for them, and re-layouts  3.92 us (6%)
  between operations  1.01 us (1%)
    pallas_call x1, Pallas kernels, on_device(): call(child_kernel, shaped(SLAB, LANES), [VMEM] * 2, HBM, [pltpu.VMEM((2 *...  15.5 us
    all_to_all x1, starting transfers between devices, on_device(): got = lax.all_to_all(packed, 'dir', split_axis=0, concat_axis=0)  8.48 us
    all_to_all x1, starting transfers between devices, on_device(): lax.all_to_all(child_rows_out.reshape(DIRS, BOXES, LANES), 'dir', split_a...  7.41 us
    all_to_all x1, starting transfers between devices, on_device(): lax.all_to_all(finer.reshape(DIRS, 2 * BOXES, LANES), 'dir', split_axis=0...  6.03 us
    pallas_call x1, Pallas kernels, on_device(): call(beside_kernel, (shaped(2 * DIRS * BOXES, LANES), shaped(LANES, 2 * L...  4.45 us
    unnamed x21, local copies, waits for them, and re-layouts  3.92 us
    all_to_all x1, waiting for transfers between devices, on_device(): got = lax.all_to_all(packed, 'dir', split_axis=0, concat_axis=0)  3.66 us
    ppermute x1, starting transfers between devices, on_device(): lax.ppermute(to_upper, 'slab', [(s, s + 1) for s in range(slabs - 1)])  3.48 us
  transfers between devices with their start and end apart: 5, of which 2 were waited for; matrix products, arithmetic and copies ran while one was open for 0% of the time, Pallas kernels for 40%

profile of v1, /device:TPU:2, one launch (start us, length us, event | category | flops | bytes accessed | tf_op | source)
XLA Modules:
  0.0 69.2 jit_solution(8045423589495204782)
XLA Ops:
  0.7 2.5 %shard_map.140 = f32[32,48,128]{2,1,0:T(8,128)} custom-call(f32[32,2,2048]{2,1,0:T(2,128)} %bitcast.32, s32[24,32]{1,0:T(8,128)} %bitcast.34, s32[24,32]{1,0:T(8,128)} %bitcast.35, s32[1,32]{1,0:T(1,128)} %parent.1, s32[1,32]{1,0:T(1,128)} %octant.1), custom_call_target="tpu_custom_call" | custom-call | flops 1048576 | bytes 3145728 | tf_op jit(solution)/shard_map/pallas_call | solution.py:397
  3.2 8.5 %all-to-all-start = ((f32[32,48,128]{2,1,0:T(8,128)}), f32[32,48,128]{2,1,0:T(8,128)S(1)}, u32[]{:S(2)}, u32[]{:S(2)}) async-start(f32[32,48,128]{2,1,0:T(8,128)} %shard_map.140), calls=%async_computation | async-start | bytes 1572864 | tf_op jit(solution)/shard_map/all_to_all | solution.py:421
  11.7 0.1 copy.15.theta
  11.8 4.4 %shard_map.141 = (f32[2048,128]{1,0:T(8,128)}, f32[128,256]{1,0:T(8,128)S(1)}, f32[6,512,512]{2,1,0:T(8,128)S(1)}, bf16[6,256,512]{2,1,0:T(8,128)(2,1)S(1)}) custom-call(s32[1]{0:T(128)} %bitcast.6.me, f32[1536,128]{1,0:T(8,128)} %bitcast.7.packed, f32[64,32]{1,0:T(8,128)S(1)} %copy.15.theta, f32[160,2,2048]{2,1,0:T(2,128)} %child.1, ...), custom_call_target="tpu_custom_call" | custom-call | flops 1073741824 | bytes 4194304 | tf_op jit(solution)/shard_map/pallas_call | solution.py:424
  16.2 2.7 %copy-done.4 = f32[6,512,512]{2,1,0:T(8,128)} copy-done((f32[6,512,512]{2,1,0:T(8,128)}, f32[6,512,512]{2,1,0:T(8,128)S(1)}, u32[]{:S(2)}) %copy-start.4) | copy-done | bytes 6291480
  18.9 1.1 %copy-done.5 = bf16[6,256,512]{2,1,0:T(8,128)(2,1)} copy-done((bf16[6,256,512]{2,1,0:T(8,128)(2,1)}, bf16[6,256,512]{2,1,0:T(8,128)(2,1)S(1)}, u32[]{:S(2)}) %copy-start.5) | copy-done | bytes 1572888
  20.0 3.7 %all-to-all-done = f32[32,48,128]{2,1,0:T(8,128)S(1)} async-done(((f32[32,48,128]{2,1,0:T(8,128)}), f32[32,48,128]{2,1,0:T(8,128)S(1)}, u32[]{:S(2)}, u32[]{:S(2)}) %all-to-all-start) | async-done | bytes 786464 | tf_op jit(solution)/shard_map/all_to_all | solution.py:421
  23.7 6.0 %all-to-all-start.2 = ((f32[32,64,128]{2,1,0:T(8,128)}), f32[32,64,128]{2,1,0:T(8,128)S(1)}, u32[]{:S(2)}, u32[]{:S(2)}) async-start(f32[32,64,128]{2,1,0:T(8,128)} %bitcast.14), calls=%async_computation.2 | async-start | bytes 2097152 | tf_op jit(solution)/shard_map/all_to_all | solution.py:447
  29.7 0.0 copy-start
  29.7 0.0 copy-start.3
  29.8 15.5 %shard_map.142 = f32[1024,128]{1,0:T(8,128)} custom-call(f32[1536,128]{1,0:T(8,128)S(1)} %bitcast.22, f32[128,256]{1,0:T(8,128)S(1)} %get-tuple-element.8.table), custom_call_target="tpu_custom_call" | custom-call | flops 17179869184 | bytes 4194304 | tf_op jit(solution)/shard_map/pallas_call | solution.py:449
  45.3 0.0 all-to-all-done.2.got
  45.3 7.4 %all-to-all-start.1 = ((f32[32,32,128]{2,1,0:T(8,128)}), f32[32,32,128]{2,1,0:T(8,128)S(1)}, u32[]{:S(2)}, u32[]{:S(2)}) async-start(f32[32,32,128]{2,1,0:T(8,128)} %bitcast.12), calls=%async_computation.1 | async-start | bytes 1048576 | tf_op jit(solution)/shard_map/all_to_all | solution.py:465
  52.7 0.0 slice-start
  52.7 1.9 %shard_map.145 = (f32[32,512]{1,0:T(8,128)S(1)}, f32[32,512]{1,0:T(8,128)S(1)}) custom-call(s32[1]{0:T(128)} %bitcast.6.me, f32[32,64,128]{2,1,0:T(8,128)S(1)} %all-to-all-done.2.got, f32[1536,128]{1,0:T(8,128)S(1)} %bitcast.23, f32[64,128]{1,0:T(8,128)S(1)} %bitcast.25, f32[8,2,8192]{2,1,0:T(2,128)} %shift_table.3, s32[2,32]{1,0:T(2,128)S(1)} %bitcast.29), custom_call_target="tpu_custom_call" | custom-call | flops 1073741824 | bytes 4194304 | tf_op jit(solution)/shard_map/pallas_call | solution.py:469
  54.6 3.5 %collective-permute-start = (f32[32,512]{1,0:T(8,128)S(1)}, f32[32,512]{1,0:T(8,128)S(1)}, u32[]{:S(2)}, u32[]{:S(2)}) collective-permute-start(f32[32,512]{1,0:T(8,128)S(1)} %get-tuple-element.10), channel_id=1, source_target_pairs={{0,1},{1,2},{2,3},{4,5},{5,6},{6,7},{8,9},{9,10},{10,11},{12,13},{... | collective-permute-start | bytes 196616 | tf_op jit(solution)/shard_map/ppermute | solution.py:488
  58.1 0.0 slice-start.1
  58.1 1.7 %collective-permute-start.1 = (f32[32,512]{1,0:T(8,128)S(1)}, f32[32,512]{1,0:T(8,128)S(1)}, u32[]{:S(2)}, u32[]{:S(2)}) collective-permute-start(f32[32,512]{1,0:T(8,128)S(1)} %get-tuple-element.11), channel_id=1, source_target_pairs={{1,0},{2,1},{3,2},{5,4},{6,5},{7,6},{9,8},{10,9},{11,10},{13,12},{... | collective-permute-start | bytes 196616 | tf_op jit(solution)/shard_map/ppermute | solution.py:489
  59.9 2.7 %shard_map.144.own = f32[128,512]{1,0:T(8,128)S(1)} custom-call(s32[1]{0:T(128)} %bitcast.6.me, f32[32,64,128]{2,1,0:T(8,128)S(1)} %all-to-all-done.2.got, f32[1536,128]{1,0:T(8,128)S(1)} %bitcast.24, f32[64,128]{1,0:T(8,128)S(1)} %bitcast.26, f32[8,2,8192]{2,1,0:T(2,128)} %shift_table.3), custom_call_target="tpu_custom_call" | custom-call | flops 2147483648 | bytes 4194304 | tf_op jit(solution)/shard_map/pallas_call | solution.py:478
  62.6 0.0 collective-permute-done.lower
  62.6 2.0 %collective-permute-done.1.upper = f32[32,512]{1,0:T(8,128)S(1)} collective-permute-done((f32[32,512]{1,0:T(8,128)S(1)}, f32[32,512]{1,0:T(8,128)S(1)}, u32[]{:S(2)}, u32[]{:S(2)}) %collective-permute-start.1) | collective-permute-done | bytes 65568 | tf_op jit(solution)/shard_map/ppermute | solution.py:489
  64.6 3.2 %shard_map.146 = f32[128,2,256]{2,1,0:T(2,128)} custom-call(f32[128,512]{1,0:T(8,128)S(1)} %shard_map.144.own, f32[32,512]{1,0:T(8,128)S(1)} %collective-permute-done.lower, f32[32,512]{1,0:T(8,128)S(1)} %collective-permute-done.1.upper, f32[6,512,512]{2,1,0:T(8,128)S(1)} %bitcast.31, bf16[6,256,512]{2,1,0:T(8,128)(2,1)S(1)} %copy-done.6), custom_call_target="tpu_custom_call" | custom-call | flops 4294967296 | bytes 8388608 | tf_op jit(solution)/shard_map/pallas_call | solution.py:501
  67.8 0.0 all-to-all-done.1.got
  67.8 1.3 %shard_map.143 = f32[32,2,2048]{2,1,0:T(2,128)} custom-call(f32[32,32,128]{2,1,0:T(8,128)S(1)} %all-to-all-done.1.got), custom_call_target="tpu_custom_call" | custom-call | flops 1048576 | bytes 2097152 | tf_op jit(solution)/shard_map/pallas_call | solution.py:491
  (15 shorter events, 0.0 us)
Async XLA Ops:
  0.6 11.0 %copy-start.7 = (f32[64,32]{0,1:T(8,128)S(1)}, f32[64,32]{0,1:T(8,128)}, u32[]{:S(2)}) copy-start(f32[64,32]{0,1:T(8,128)} %param.19) | copy-start | bytes 24580
  0.6 11.1 %copy-start.1 = (s32[1,128,24]{1,2,0:T(8,128)S(1)}, s32[1,128,24]{1,2,0:T(8,128)}, u32[]{:S(2)}) copy-start(s32[1,128,24]{1,2,0:T(8,128)} %param.24) | copy-start | bytes 36868
  0.7 11.1 %copy-start.2 = (s32[1,128,24]{1,2,0:T(8,128)S(1)}, s32[1,128,24]{1,2,0:T(8,128)}, u32[]{:S(2)}) copy-start(s32[1,128,24]{1,2,0:T(8,128)} %param.23) | copy-start | bytes 36868
  3.2 20.5 %all-to-all-start = ((f32[32,48,128]{2,1,0:T(8,128)}), f32[32,48,128]{2,1,0:T(8,128)S(1)}, u32[]{:S(2)}, u32[]{:S(2)}) async-start(f32[32,48,128]{2,1,0:T(8,128)} %shard_map.140), calls=%async_computation | async-start | bytes 1572864 | tf_op jit(solution)/shard_map/all_to_all | solution.py:421
  16.2 2.7 %copy-start.4 = (f32[6,512,512]{2,1,0:T(8,128)}, f32[6,512,512]{2,1,0:T(8,128)S(1)}, u32[]{:S(2)}) copy-start(f32[6,512,512]{2,1,0:T(8,128)S(1)} %get-tuple-element.12.weights) | copy-start | bytes 18874372
  18.9 1.1 %copy-start.5 = (bf16[6,256,512]{2,1,0:T(8,128)(2,1)}, bf16[6,256,512]{2,1,0:T(8,128)(2,1)S(1)}, u32[]{:S(2)}) copy-start(bf16[6,256,512]{2,1,0:T(8,128)(2,1)S(1)} %get-tuple-element.13.hots) | copy-start | bytes 4718596
  23.7 21.6 %all-to-all-start.2 = ((f32[32,64,128]{2,1,0:T(8,128)}), f32[32,64,128]{2,1,0:T(8,128)S(1)}, u32[]{:S(2)}, u32[]{:S(2)}) async-start(f32[32,64,128]{2,1,0:T(8,128)} %bitcast.14), calls=%async_computation.2 | async-start | bytes 2097152 | tf_op jit(solution)/shard_map/all_to_all | solution.py:447
  29.7 23.0 %copy-start = (f32[128,64]{0,1:T(8,128)S(1)}, f32[128,64]{0,1:T(8,128)}, u32[]{:S(2)}) copy-start(f32[128,64]{0,1:T(8,128)} %param.20) | copy-start | bytes 98308
  29.7 23.0 %copy-start.3 = (s32[1,2,32]{2,1,0:T(2,128)S(1)}, s32[1,2,32]{2,1,0:T(2,128)}, u32[]{:S(2)}) copy-start(s32[1,2,32]{2,1,0:T(2,128)} %param.22) | copy-start | bytes 772
  45.3 22.5 %all-to-all-start.1 = ((f32[32,32,128]{2,1,0:T(8,128)}), f32[32,32,128]{2,1,0:T(8,128)S(1)}, u32[]{:S(2)}, u32[]{:S(2)}) async-start(f32[32,32,128]{2,1,0:T(8,128)} %bitcast.12), calls=%async_computation.1 | async-start | bytes 1048576 | tf_op jit(solution)/shard_map/all_to_all | solution.py:465
  52.7 11.8 %slice-start = ((s8[6291456]{0:T(1024)(128)(4,1)}), s8[4194304]{0:T(1024)(128)(4,1)S(1)}, s32[]{:S(2)}) async-start(s8[6291456]{0:T(1024)(128)(4,1)} %bitcast.30), calls=%async_computation.3 | async-start | bytes 8388608
  54.6 7.9 %collective-permute-start = (f32[32,512]{1,0:T(8,128)S(1)}, f32[32,512]{1,0:T(8,128)S(1)}, u32[]{:S(2)}, u32[]{:S(2)}) collective-permute-start(f32[32,512]{1,0:T(8,128)S(1)} %get-tuple-element.10), channel_id=1, source_target_pairs={{0,1},{1,2},{2,3},{4,5},{5,6},{6,7},{8,9},{9,10},{10,11},{12,13},{... | collective-permute-start | bytes 196616 | tf_op jit(solution)/shard_map/ppermute | solution.py:488
  58.1 6.4 %slice-start.1 = ((s8[6291456]{0:T(1024)(128)(4,1)}), s8[2097152]{0:T(1024)(128)(4,1)S(1)}, s32[]{:S(2)}) async-start(s8[6291456]{0:T(1024)(128)(4,1)} %bitcast.30), calls=%async_computation.4 | async-start | bytes 4194304
  58.1 6.4 %copy-start.6 = (bf16[6,256,512]{2,1,0:T(8,128)(2,1)S(1)}, bf16[6,256,512]{2,1,0:T(8,128)(2,1)}, u32[]{:S(2)}) copy-start(bf16[6,256,512]{2,1,0:T(8,128)(2,1)} %copy-done.5) | copy-start | bytes 4718596
  58.1 6.4 %collective-permute-start.1 = (f32[32,512]{1,0:T(8,128)S(1)}, f32[32,512]{1,0:T(8,128)S(1)}, u32[]{:S(2)}, u32[]{:S(2)}) collective-permute-start(f32[32,512]{1,0:T(8,128)S(1)} %get-tuple-element.11), channel_id=1, source_target_pairs={{1,0},{2,1},{3,2},{5,4},{6,5},{7,6},{9,8},{10,9},{11,10},{13,12},{... | collective-permute-start | bytes 196616 | tf_op jit(solution)/shard_map/ppermute | solution.py:489

commit v2 on v1

--- a/solution.py
+++ b/solution.py
@@ -16,9 +16,9 @@
 BOXES = 32
 SLAB = DIRS * BOXES
 ENTRIES = 24
-TOGETHER = 4
+TOGETHER = 8
 GROUPS = ENTRIES // TOGETHER
-AT_ONCE = 8
+AT_ONCE = 12
 TYPES = 160
 PARENTS = 128
 BORDER = 32
@@ -231,7 +231,7 @@
             wanted, kinds = flat_rows(src[entry]), kind[entry]
             picked = []
             for k in range(SLAB // tile):
-                if n % 2 == 1 and k == SLAB // tile - 1:
+                if n % 3 != 0 and k == SLAB // tile - 1:
                     picked.extend(pick(exact, wanted[:, at : at + LANES]) for at in (k * tile, k * tile + LANES))
                     continue
                 hot = one_hot(SLAB, wanted[:, k * tile : (k + 1) * tile])

time: 69.7 us -> 68.7 us (0.986)
  Pallas kernels: 31.5 us -> 30.7 us
    pallas_call x1, Pallas kernels: 15.5 us -> 14.6 us  [on_device(): call(child_kernel, shaped(SLAB, LANES), [VMEM] * 2, HBM, [pltpu.VMEM((2 *...]
  transfers between devices with their start and end apart: 5 -> 5, of which waited for: 2 -> 2; matrix products, arithmetic and copies ran while one was open for 0% -> 0% of each run, Pallas kernels for 40% -> 39%
where the time goes in v2:
time: 68.7 us; the launch traced here: 68.2 us
  Pallas kernels  30.7 us (45%)
  starting transfers between devices  26.9 us (39%)
  waiting for transfers between devices  5.64 us (8%)
  local copies, waits for them, and re-layouts  3.92 us (6%)
  between operations  1.01 us (1%)
    pallas_call x1, Pallas kernels, on_device(): call(child_kernel, shaped(SLAB, LANES), [VMEM] * 2, HBM, [pltpu.VMEM((2 *...  14.6 us
    all_to_all x1, starting transfers between devices, on_device(): got = lax.all_to_all(packed, 'dir', split_axis=0, concat_axis=0)  8.48 us
    all_to_all x1, starting transfers between devices, on_device(): lax.all_to_all(child_rows_out.reshape(DIRS, BOXES, LANES), 'dir', split_a...  7.39 us
    all_to_all x1, starting transfers between devices, on_device(): lax.all_to_all(finer.reshape(DIRS, 2 * BOXES, LANES), 'dir', split_axis=0...  6.03 us
    pallas_call x1, Pallas kernels, on_device(): call(beside_kernel, (shaped(2 * DIRS * BOXES, LANES), shaped(LANES, 2 * L...  4.64 us
    unnamed x21, local copies, waits for them, and re-layouts  3.92 us
    ppermute x1, starting transfers between devices, on_device(): lax.ppermute(to_upper, 'slab', [(s, s + 1) for s in range(slabs - 1)])  3.48 us
    all_to_all x1, waiting for transfers between devices, on_device(): got = lax.all_to_all(packed, 'dir', split_axis=0, concat_axis=0)  3.46 us
  transfers between devices with their start and end apart: 5, of which 2 were waited for; matrix products, arithmetic and copies ran while one was open for 0% of the time, Pallas kernels for 39%

profile of v2, /device:TPU:2, one launch (start us, length us, event | category | flops | bytes accessed | tf_op | source)
XLA Modules:
  0.0 68.2 jit_solution(4285937840445975815)
XLA Ops:
  0.7 2.5 %shard_map.140 = f32[32,48,128]{2,1,0:T(8,128)} custom-call(f32[32,2,2048]{2,1,0:T(2,128)} %bitcast.32, s32[24,32]{1,0:T(8,128)} %bitcast.34, s32[24,32]{1,0:T(8,128)} %bitcast.35, s32[1,32]{1,0:T(1,128)} %parent.1, s32[1,32]{1,0:T(1,128)} %octant.1), custom_call_target="tpu_custom_call" | custom-call | flops 1048576 | bytes 3145728 | tf_op jit(solution)/shard_map/pallas_call | solution.py:397
  3.2 8.5 %all-to-all-start = ((f32[32,48,128]{2,1,0:T(8,128)}), f32[32,48,128]{2,1,0:T(8,128)S(1)}, u32[]{:S(2)}, u32[]{:S(2)}) async-start(f32[32,48,128]{2,1,0:T(8,128)} %shard_map.140), calls=%async_computation | async-start | bytes 1572864 | tf_op jit(solution)/shard_map/all_to_all | solution.py:421
  11.7 0.1 copy.15.theta
  11.8 4.6 %shard_map.141 = (f32[2048,128]{1,0:T(8,128)}, f32[128,256]{1,0:T(8,128)S(1)}, f32[3,512,1024]{2,1,0:T(8,128)S(1)}, bf16[3,256,1024]{2,1,0:T(8,128)(2,1)S(1)}) custom-call(s32[1]{0:T(128)} %bitcast.6.me, f32[1536,128]{1,0:T(8,128)} %bitcast.7.packed, f32[64,32]{1,0:T(8,128)S(1)} %copy.15.theta, f32[160,2,2048]{2,1,0:T(2,128)} %child.1, ...), custom_call_target="tpu_custom_call" | custom-call | flops 1073741824 | bytes 4194304 | tf_op jit(solution)/shard_map/pallas_call | solution.py:424
  16.4 2.7 %copy-done.4 = f32[3,512,1024]{2,1,0:T(8,128)} copy-done((f32[3,512,1024]{2,1,0:T(8,128)}, f32[3,512,1024]{2,1,0:T(8,128)S(1)}, u32[]{:S(2)}) %copy-start.4) | copy-done | bytes 6291480
  19.1 1.1 %copy-done.5 = bf16[3,256,1024]{2,1,0:T(8,128)(2,1)} copy-done((bf16[3,256,1024]{2,1,0:T(8,128)(2,1)}, bf16[3,256,1024]{2,1,0:T(8,128)(2,1)S(1)}, u32[]{:S(2)}) %copy-start.5) | copy-done | bytes 1572888
  20.2 3.5 %all-to-all-done = f32[32,48,128]{2,1,0:T(8,128)S(1)} async-done(((f32[32,48,128]{2,1,0:T(8,128)}), f32[32,48,128]{2,1,0:T(8,128)S(1)}, u32[]{:S(2)}, u32[]{:S(2)}) %all-to-all-start) | async-done | bytes 786464 | tf_op jit(solution)/shard_map/all_to_all | solution.py:421
  23.7 6.0 %all-to-all-start.2 = ((f32[32,64,128]{2,1,0:T(8,128)}), f32[32,64,128]{2,1,0:T(8,128)S(1)}, u32[]{:S(2)}, u32[]{:S(2)}) async-start(f32[32,64,128]{2,1,0:T(8,128)} %bitcast.14), calls=%async_computation.2 | async-start | bytes 2097152 | tf_op jit(solution)/shard_map/all_to_all | solution.py:447
  29.7 0.0 copy-start
  29.7 0.0 copy-start.3
  29.8 14.6 %shard_map.142 = f32[1024,128]{1,0:T(8,128)} custom-call(f32[1536,128]{1,0:T(8,128)S(1)} %bitcast.22, f32[128,256]{1,0:T(8,128)S(1)} %get-tuple-element.8.table), custom_call_target="tpu_custom_call" | custom-call | flops 17179869184 | bytes 4194304 | tf_op jit(solution)/shard_map/pallas_call | solution.py:449
  44.4 0.0 all-to-all-done.2.got
  44.4 7.4 %all-to-all-start.1 = ((f32[32,32,128]{2,1,0:T(8,128)}), f32[32,32,128]{2,1,0:T(8,128)S(1)}, u32[]{:S(2)}, u32[]{:S(2)}) async-start(f32[32,32,128]{2,1,0:T(8,128)} %bitcast.12), calls=%async_computation.1 | async-start | bytes 1048576 | tf_op jit(solution)/shard_map/all_to_all | solution.py:465
  51.8 0.0 slice-start
  51.8 1.9 %shard_map.145 = (f32[32,512]{1,0:T(8,128)S(1)}, f32[32,512]{1,0:T(8,128)S(1)}) custom-call(s32[1]{0:T(128)} %bitcast.6.me, f32[32,64,128]{2,1,0:T(8,128)S(1)} %all-to-all-done.2.got, f32[1536,128]{1,0:T(8,128)S(1)} %bitcast.23, f32[64,128]{1,0:T(8,128)S(1)} %bitcast.25, f32[8,2,8192]{2,1,0:T(2,128)} %shift_table.3, s32[2,32]{1,0:T(2,128)S(1)} %bitcast.29), custom_call_target="tpu_custom_call" | custom-call | flops 1073741824 | bytes 4194304 | tf_op jit(solution)/shard_map/pallas_call | solution.py:469
  53.7 3.5 %collective-permute-start = (f32[32,512]{1,0:T(8,128)S(1)}, f32[32,512]{1,0:T(8,128)S(1)}, u32[]{:S(2)}, u32[]{:S(2)}) collective-permute-start(f32[32,512]{1,0:T(8,128)S(1)} %get-tuple-element.10), channel_id=1, source_target_pairs={{0,1},{1,2},{2,3},{4,5},{5,6},{6,7},{8,9},{9,10},{10,11},{12,13},{... | collective-permute-start | bytes 196616 | tf_op jit(solution)/shard_map/ppermute | solution.py:488
  57.2 0.0 slice-start.1
  57.2 1.6 %collective-permute-start.1 = (f32[32,512]{1,0:T(8,128)S(1)}, f32[32,512]{1,0:T(8,128)S(1)}, u32[]{:S(2)}, u32[]{:S(2)}) collective-permute-start(f32[32,512]{1,0:T(8,128)S(1)} %get-tuple-element.11), channel_id=1, source_target_pairs={{1,0},{2,1},{3,2},{5,4},{6,5},{7,6},{9,8},{10,9},{11,10},{13,12},{... | collective-permute-start | bytes 196616 | tf_op jit(solution)/shard_map/ppermute | solution.py:489
  58.8 2.7 %shard_map.144.own = f32[128,512]{1,0:T(8,128)S(1)} custom-call(s32[1]{0:T(128)} %bitcast.6.me, f32[32,64,128]{2,1,0:T(8,128)S(1)} %all-to-all-done.2.got, f32[1536,128]{1,0:T(8,128)S(1)} %bitcast.24, f32[64,128]{1,0:T(8,128)S(1)} %bitcast.26, f32[8,2,8192]{2,1,0:T(2,128)} %shift_table.3), custom_call_target="tpu_custom_call" | custom-call | flops 2147483648 | bytes 4194304 | tf_op jit(solution)/shard_map/pallas_call | solution.py:478
  61.4 0.0 collective-permute-done.lower
  61.4 2.2 %collective-permute-done.1.upper = f32[32,512]{1,0:T(8,128)S(1)} collective-permute-done((f32[32,512]{1,0:T(8,128)S(1)}, f32[32,512]{1,0:T(8,128)S(1)}, u32[]{:S(2)}, u32[]{:S(2)}) %collective-permute-start.1) | collective-permute-done | bytes 65568 | tf_op jit(solution)/shard_map/ppermute | solution.py:489
  63.6 3.1 %shard_map.146 = f32[128,2,256]{2,1,0:T(2,128)} custom-call(f32[128,512]{1,0:T(8,128)S(1)} %shard_map.144.own, f32[32,512]{1,0:T(8,128)S(1)} %collective-permute-done.lower, f32[32,512]{1,0:T(8,128)S(1)} %collective-permute-done.1.upper, f32[3,512,1024]{2,1,0:T(8,128)S(1)} %bitcast.31, bf16[3,256,1024]{2,1,0:T(8,128)(2,1)S(1)} %copy-done.6), custom_call_target="tpu_custom_call" | custom-call | flops 4294967296 | bytes 8388608 | tf_op jit(solution)/shard_map/pallas_call | solution.py:501
  66.8 0.0 all-to-all-done.1.got
  66.8 1.3 %shard_map.143 = f32[32,2,2048]{2,1,0:T(2,128)} custom-call(f32[32,32,128]{2,1,0:T(8,128)S(1)} %all-to-all-done.1.got), custom_call_target="tpu_custom_call" | custom-call | flops 1048576 | bytes 2097152 | tf_op jit(solution)/shard_map/pallas_call | solution.py:491
  (15 shorter events, 0.0 us)
Async XLA Ops:
  0.6 11.0 %copy-start.7 = (f32[64,32]{0,1:T(8,128)S(1)}, f32[64,32]{0,1:T(8,128)}, u32[]{:S(2)}) copy-start(f32[64,32]{0,1:T(8,128)} %param.19) | copy-start | bytes 24580
  0.6 11.1 %copy-start.1 = (s32[1,128,24]{1,2,0:T(8,128)S(1)}, s32[1,128,24]{1,2,0:T(8,128)}, u32[]{:S(2)}) copy-start(s32[1,128,24]{1,2,0:T(8,128)} %param.24) | copy-start | bytes 36868
  0.7 11.1 %copy-start.2 = (s32[1,128,24]{1,2,0:T(8,128)S(1)}, s32[1,128,24]{1,2,0:T(8,128)}, u32[]{:S(2)}) copy-start(s32[1,128,24]{1,2,0:T(8,128)} %param.23) | copy-start | bytes 36868
  3.2 20.5 %all-to-all-start = ((f32[32,48,128]{2,1,0:T(8,128)}), f32[32,48,128]{2,1,0:T(8,128)S(1)}, u32[]{:S(2)}, u32[]{:S(2)}) async-start(f32[32,48,128]{2,1,0:T(8,128)} %shard_map.140), calls=%async_computation | async-start | bytes 1572864 | tf_op jit(solution)/shard_map/all_to_all | solution.py:421
  16.4 2.7 %copy-start.4 = (f32[3,512,1024]{2,1,0:T(8,128)}, f32[3,512,1024]{2,1,0:T(8,128)S(1)}, u32[]{:S(2)}) copy-start(f32[3,512,1024]{2,1,0:T(8,128)S(1)} %get-tuple-element.12.weights) | copy-start | bytes 18874372
  19.1 1.1 %copy-start.5 = (bf16[3,256,1024]{2,1,0:T(8,128)(2,1)}, bf16[3,256,1024]{2,1,0:T(8,128)(2,1)S(1)}, u32[]{:S(2)}) copy-start(bf16[3,256,1024]{2,1,0:T(8,128)(2,1)S(1)} %get-tuple-element.13.hots) | copy-start | bytes 4718596
  23.7 20.7 %all-to-all-start.2 = ((f32[32,64,128]{2,1,0:T(8,128)}), f32[32,64,128]{2,1,0:T(8,128)S(1)}, u32[]{:S(2)}, u32[]{:S(2)}) async-start(f32[32,64,128]{2,1,0:T(8,128)} %bitcast.14), calls=%async_computation.2 | async-start | bytes 2097152 | tf_op jit(solution)/shard_map/all_to_all | solution.py:447
  29.7 22.0 %copy-start = (f32[128,64]{0,1:T(8,128)S(1)}, f32[128,64]{0,1:T(8,128)}, u32[]{:S(2)}) copy-start(f32[128,64]{0,1:T(8,128)} %param.20) | copy-start | bytes 98308
  29.7 22.0 %copy-start.3 = (s32[1,2,32]{2,1,0:T(2,128)S(1)}, s32[1,2,32]{2,1,0:T(2,128)}, u32[]{:S(2)}) copy-start(s32[1,2,32]{2,1,0:T(2,128)} %param.22) | copy-start | bytes 772
  44.4 22.4 %all-to-all-start.1 = ((f32[32,32,128]{2,1,0:T(8,128)}), f32[32,32,128]{2,1,0:T(8,128)S(1)}, u32[]{:S(2)}, u32[]{:S(2)}) async-start(f32[32,32,128]{2,1,0:T(8,128)} %bitcast.12), calls=%async_computation.1 | async-start | bytes 1048576 | tf_op jit(solution)/shard_map/all_to_all | solution.py:465
  51.8 11.8 %slice-start = ((s8[6291456]{0:T(1024)(128)(4,1)}), s8[4194304]{0:T(1024)(128)(4,1)S(1)}, s32[]{:S(2)}) async-start(s8[6291456]{0:T(1024)(128)(4,1)} %bitcast.30), calls=%async_computation.3 | async-start | bytes 8388608
  53.7 7.7 %collective-permute-start = (f32[32,512]{1,0:T(8,128)S(1)}, f32[32,512]{1,0:T(8,128)S(1)}, u32[]{:S(2)}, u32[]{:S(2)}) collective-permute-start(f32[32,512]{1,0:T(8,128)S(1)} %get-tuple-element.10), channel_id=1, source_target_pairs={{0,1},{1,2},{2,3},{4,5},{5,6},{6,7},{8,9},{9,10},{10,11},{12,13},{... | collective-permute-start | bytes 196616 | tf_op jit(solution)/shard_map/ppermute | solution.py:488
  57.2 6.4 %slice-start.1 = ((s8[6291456]{0:T(1024)(128)(4,1)}), s8[2097152]{0:T(1024)(128)(4,1)S(1)}, s32[]{:S(2)}) async-start(s8[6291456]{0:T(1024)(128)(4,1)} %bitcast.30), calls=%async_computation.4 | async-start | bytes 4194304
  57.2 6.4 %copy-start.6 = (bf16[3,256,1024]{2,1,0:T(8,128)(2,1)S(1)}, bf16[3,256,1024]{2,1,0:T(8,128)(2,1)}, u32[]{:S(2)}) copy-start(bf16[3,256,1024]{2,1,0:T(8,128)(2,1)} %copy-done.5) | copy-start | bytes 4718596
  57.2 6.4 %collective-permute-start.1 = (f32[32,512]{1,0:T(8,128)S(1)}, f32[32,512]{1,0:T(8,128)S(1)}, u32[]{:S(2)}, u32[]{:S(2)}) collective-permute-start(f32[32,512]{1,0:T(8,128)S(1)} %get-tuple-element.11), channel_id=1, source_target_pairs={{1,0},{2,1},{3,2},{5,4},{6,5},{7,6},{9,8},{10,9},{11,10},{13,12},{... | collective-permute-start | bytes 196616 | tf_op jit(solution)/shard_map/ppermute | solution.py:489

commit v3 on v2

--- a/solution.py
+++ b/solution.py
@@ -339,8 +339,8 @@
     copy.wait()
     (real0, imag0), (real1, imag1) = shifted_sums(hot, got, turn, shifts, count)
     for m, value in enumerate((real0, real1, imag0, imag1)):
-        up[:, m * LANES : (m + 1) * LANES] = value[:BORDER]
-        down[:, m * LANES : (m + 1) * LANES] = value[BORDER:]
+        up[m * BORDER : (m + 1) * BORDER, :] = value[:BORDER]
+        down[m * BORDER : (m + 1) * BORDER, :] = value[BORDER:]
 
 
 def own_kernel(me, got, owner, turn, shift_table, out, shifts, sem):
@@ -354,10 +354,11 @@
 
 
 def parent_kernel(own, lower, upper, weights, hots, out):
-    border = jnp.concatenate([lower[...], upper[...], jnp.zeros((2 * BORDER, 4 * LANES), F32)], axis=0)
+    none = jnp.zeros((2 * BORDER, LANES), F32)
     fields = []
     for m in range(4):
-        turned = jnp.transpose(border[:, m * LANES : (m + 1) * LANES])
+        cut = slice(m * BORDER, (m + 1) * BORDER)
+        turned = jnp.transpose(jnp.concatenate([lower[cut, :], upper[cut, :], none], axis=0))
         fields.append(jnp.concatenate([own[:, m * PARENTS : (m + 1) * PARENTS], turned], axis=1))
     fields = jnp.concatenate(split(jnp.concatenate(fields, axis=0)), axis=0)
     rows = 4 * LANES
@@ -468,7 +469,7 @@
     (shift_rows,) = kept_out(shift_table)
     to_upper, to_lower = call(
         border_kernel,
-        (shaped(BORDER, 4 * LANES),) * 2,
+        (shaped(4 * BORDER, LANES),) * 2,
         [SMEM, VMEM, VMEM, VMEM, HBM, VMEM],
         (VMEM,) * 2,
         [pltpu.VMEM((OCTANTS, 2, 2 * LANES), F32), DMA],

time: 68.7 us -> 68.7 us (level)
  no operation moved by 1% of the time
where the time goes in v3:
time: 68.7 us; the launch traced here: 68.2 us
  Pallas kernels  30.7 us (45%)
  starting transfers between devices  26.9 us (39%)
  waiting for transfers between devices  5.64 us (8%)
  local copies, waits for them, and re-layouts  3.92 us (6%)
  between operations  1.01 us (1%)
    pallas_call x1, Pallas kernels, on_device(): call(child_kernel, shaped(SLAB, LANES), [VMEM] * 2, HBM, [pltpu.VMEM((2 *...  14.6 us
    all_to_all x1, starting transfers between devices, on_device(): got = lax.all_to_all(packed, 'dir', split_axis=0, concat_axis=0)  8.48 us
    all_to_all x1, starting transfers between devices, on_device(): lax.all_to_all(child_rows_out.reshape(DIRS, BOXES, LANES), 'dir', split_a...  7.39 us
    all_to_all x1, starting transfers between devices, on_device(): lax.all_to_all(finer.reshape(DIRS, 2 * BOXES, LANES), 'dir', split_axis=0...  6.03 us
    pallas_call x1, Pallas kernels, on_device(): call(beside_kernel, (shaped(2 * DIRS * BOXES, LANES), shaped(LANES, 2 * L...  4.64 us
    unnamed x21, local copies, waits for them, and re-layouts  3.92 us
    ppermute x1, starting transfers between devices, on_device(): lax.ppermute(to_upper, 'slab', [(s, s + 1) for s in range(slabs - 1)])  3.48 us
    all_to_all x1, waiting for transfers between devices, on_device(): got = lax.all_to_all(packed, 'dir', split_axis=0, concat_axis=0)  3.46 us
  transfers between devices with their start and end apart: 5, of which 2 were waited for; matrix products, arithmetic and copies ran while one was open for 0% of the time, Pallas kernels for 39%

profile of v3, /device:TPU:2, one launch (start us, length us, event | category | flops | bytes accessed | tf_op | source)
XLA Modules:
  0.0 68.2 jit_solution(854387105852570604)
XLA Ops:
  0.7 2.5 %shard_map.140 = f32[32,48,128]{2,1,0:T(8,128)} custom-call(f32[32,2,2048]{2,1,0:T(2,128)} %bitcast.32, s32[24,32]{1,0:T(8,128)} %bitcast.34, s32[24,32]{1,0:T(8,128)} %bitcast.35, s32[1,32]{1,0:T(1,128)} %parent.1, s32[1,32]{1,0:T(1,128)} %octant.1), custom_call_target="tpu_custom_call" | custom-call | flops 1048576 | bytes 3145728 | tf_op jit(solution)/shard_map/pallas_call | solution.py:398
  3.2 8.5 %all-to-all-start = ((f32[32,48,128]{2,1,0:T(8,128)}), f32[32,48,128]{2,1,0:T(8,128)S(1)}, u32[]{:S(2)}, u32[]{:S(2)}) async-start(f32[32,48,128]{2,1,0:T(8,128)} %shard_map.140), calls=%async_computation | async-start | bytes 1572864 | tf_op jit(solution)/shard_map/all_to_all | solution.py:422
  11.7 0.1 copy.15.theta
  11.8 4.6 %shard_map.141 = (f32[2048,128]{1,0:T(8,128)}, f32[128,256]{1,0:T(8,128)S(1)}, f32[3,512,1024]{2,1,0:T(8,128)S(1)}, bf16[3,256,1024]{2,1,0:T(8,128)(2,1)S(1)}) custom-call(s32[1]{0:T(128)} %bitcast.6.me, f32[1536,128]{1,0:T(8,128)} %bitcast.7.packed, f32[64,32]{1,0:T(8,128)S(1)} %copy.15.theta, f32[160,2,2048]{2,1,0:T(2,128)} %child.1, ...), custom_call_target="tpu_custom_call" | custom-call | flops 1073741824 | bytes 4194304 | tf_op jit(solution)/shard_map/pallas_call | solution.py:425
  16.4 2.7 %copy-done.4 = f32[3,512,1024]{2,1,0:T(8,128)} copy-done((f32[3,512,1024]{2,1,0:T(8,128)}, f32[3,512,1024]{2,1,0:T(8,128)S(1)}, u32[]{:S(2)}) %copy-start.4) | copy-done | bytes 6291480
  19.1 1.1 %copy-done.5 = bf16[3,256,1024]{2,1,0:T(8,128)(2,1)} copy-done((bf16[3,256,1024]{2,1,0:T(8,128)(2,1)}, bf16[3,256,1024]{2,1,0:T(8,128)(2,1)S(1)}, u32[]{:S(2)}) %copy-start.5) | copy-done | bytes 1572888
  20.2 3.5 %all-to-all-done = f32[32,48,128]{2,1,0:T(8,128)S(1)} async-done(((f32[32,48,128]{2,1,0:T(8,128)}), f32[32,48,128]{2,1,0:T(8,128)S(1)}, u32[]{:S(2)}, u32[]{:S(2)}) %all-to-all-start) | async-done | bytes 786464 | tf_op jit(solution)/shard_map/all_to_all | solution.py:422
  23.7 6.0 %all-to-all-start.2 = ((f32[32,64,128]{2,1,0:T(8,128)}), f32[32,64,128]{2,1,0:T(8,128)S(1)}, u32[]{:S(2)}, u32[]{:S(2)}) async-start(f32[32,64,128]{2,1,0:T(8,128)} %bitcast.14), calls=%async_computation.2 | async-start | bytes 2097152 | tf_op jit(solution)/shard_map/all_to_all | solution.py:448
  29.7 0.0 copy-start
  29.7 0.0 copy-start.3
  29.8 14.6 %shard_map.142 = f32[1024,128]{1,0:T(8,128)} custom-call(f32[1536,128]{1,0:T(8,128)S(1)} %bitcast.22, f32[128,256]{1,0:T(8,128)S(1)} %get-tuple-element.8.table), custom_call_target="tpu_custom_call" | custom-call | flops 17179869184 | bytes 4194304 | tf_op jit(solution)/shard_map/pallas_call | solution.py:450
  44.4 0.0 all-to-all-done.2.got
  44.4 7.4 %all-to-all-start.1 = ((f32[32,32,128]{2,1,0:T(8,128)}), f32[32,32,128]{2,1,0:T(8,128)S(1)}, u32[]{:S(2)}, u32[]{:S(2)}) async-start(f32[32,32,128]{2,1,0:T(8,128)} %bitcast.12), calls=%async_computation.1 | async-start | bytes 1048576 | tf_op jit(solution)/shard_map/all_to_all | solution.py:466
  51.8 0.0 slice-start
  51.8 1.9 %shard_map.145 = (f32[128,128]{1,0:T(8,128)S(1)}, f32[128,128]{1,0:T(8,128)S(1)}) custom-call(s32[1]{0:T(128)} %bitcast.6.me, f32[32,64,128]{2,1,0:T(8,128)S(1)} %all-to-all-done.2.got, f32[1536,128]{1,0:T(8,128)S(1)} %bitcast.23, f32[64,128]{1,0:T(8,128)S(1)} %bitcast.25, f32[8,2,8192]{2,1,0:T(2,128)} %shift_table.3, s32[2,32]{1,0:T(2,128)S(1)} %bitcast.29), custom_call_target="tpu_custom_call" | custom-call | flops 1073741824 | bytes 4194304 | tf_op jit(solution)/shard_map/pallas_call | solution.py:470
  53.7 3.5 %collective-permute-start = (f32[128,128]{1,0:T(8,128)S(1)}, f32[128,128]{1,0:T(8,128)S(1)}, u32[]{:S(2)}, u32[]{:S(2)}) collective-permute-start(f32[128,128]{1,0:T(8,128)S(1)} %get-tuple-element.10), channel_id=1, source_target_pairs={{0,1},{1,2},{2,3},{4,5},{5,6},{6,7},{8,9},{9,10},{10,11},{12,13},{... | collective-permute-start | bytes 196616 | tf_op jit(solution)/shard_map/ppermute | solution.py:489
  57.2 0.0 slice-start.1
  57.2 1.6 %collective-permute-start.1 = (f32[128,128]{1,0:T(8,128)S(1)}, f32[128,128]{1,0:T(8,128)S(1)}, u32[]{:S(2)}, u32[]{:S(2)}) collective-permute-start(f32[128,128]{1,0:T(8,128)S(1)} %get-tuple-element.11), channel_id=1, source_target_pairs={{1,0},{2,1},{3,2},{5,4},{6,5},{7,6},{9,8},{10,9},{11,10},{13,12},{... | collective-permute-start | bytes 196616 | tf_op jit(solution)/shard_map/ppermute | solution.py:490
  58.8 2.7 %shard_map.144.own = f32[128,512]{1,0:T(8,128)S(1)} custom-call(s32[1]{0:T(128)} %bitcast.6.me, f32[32,64,128]{2,1,0:T(8,128)S(1)} %all-to-all-done.2.got, f32[1536,128]{1,0:T(8,128)S(1)} %bitcast.24, f32[64,128]{1,0:T(8,128)S(1)} %bitcast.26, f32[8,2,8192]{2,1,0:T(2,128)} %shift_table.3), custom_call_target="tpu_custom_call" | custom-call | flops 2147483648 | bytes 4194304 | tf_op jit(solution)/shard_map/pallas_call | solution.py:479
  61.4 0.0 collective-permute-done.lower
  61.4 2.2 %collective-permute-done.1.upper = f32[128,128]{1,0:T(8,128)S(1)} collective-permute-done((f32[128,128]{1,0:T(8,128)S(1)}, f32[128,128]{1,0:T(8,128)S(1)}, u32[]{:S(2)}, u32[]{:S(2)}) %collective-permute-start.1) | collective-permute-done | bytes 65568 | tf_op jit(solution)/shard_map/ppermute | solution.py:490
  63.6 3.1 %shard_map.146 = f32[128,2,256]{2,1,0:T(2,128)} custom-call(f32[128,512]{1,0:T(8,128)S(1)} %shard_map.144.own, f32[128,128]{1,0:T(8,128)S(1)} %collective-permute-done.lower, f32[128,128]{1,0:T(8,128)S(1)} %collective-permute-done.1.upper, f32[3,512,1024]{2,1,0:T(8,128)S(1)} %bitcast.31, bf16[3,256,1024]{2,1,0:T(8,128)(2,1)S(1)} %copy-done.6), custom_call_target="tpu_custom_call" | custom-call | flops 4294967296 | bytes 8388608 | tf_op jit(solution)/shard_map/pallas_call | solution.py:502
  66.8 0.0 all-to-all-done.1.got
  66.8 1.3 %shard_map.143 = f32[32,2,2048]{2,1,0:T(2,128)} custom-call(f32[32,32,128]{2,1,0:T(8,128)S(1)} %all-to-all-done.1.got), custom_call_target="tpu_custom_call" | custom-call | flops 1048576 | bytes 2097152 | tf_op jit(solution)/shard_map/pallas_call | solution.py:492
  (15 shorter events, 0.0 us)
Async XLA Ops:
  0.6 11.0 %copy-start.7 = (f32[64,32]{0,1:T(8,128)S(1)}, f32[64,32]{0,1:T(8,128)}, u32[]{:S(2)}) copy-start(f32[64,32]{0,1:T(8,128)} %param.19) | copy-start | bytes 24580
  0.6 11.1 %copy-start.1 = (s32[1,128,24]{1,2,0:T(8,128)S(1)}, s32[1,128,24]{1,2,0:T(8,128)}, u32[]{:S(2)}) copy-start(s32[1,128,24]{1,2,0:T(8,128)} %param.24) | copy-start | bytes 36868
  0.7 11.1 %copy-start.2 = (s32[1,128,24]{1,2,0:T(8,128)S(1)}, s32[1,128,24]{1,2,0:T(8,128)}, u32[]{:S(2)}) copy-start(s32[1,128,24]{1,2,0:T(8,128)} %param.23) | copy-start | bytes 36868
  3.2 20.5 %all-to-all-start = ((f32[32,48,128]{2,1,0:T(8,128)}), f32[32,48,128]{2,1,0:T(8,128)S(1)}, u32[]{:S(2)}, u32[]{:S(2)}) async-start(f32[32,48,128]{2,1,0:T(8,128)} %shard_map.140), calls=%async_computation | async-start | bytes 1572864 | tf_op jit(solution)/shard_map/all_to_all | solution.py:422
  16.4 2.7 %copy-start.4 = (f32[3,512,1024]{2,1,0:T(8,128)}, f32[3,512,1024]{2,1,0:T(8,128)S(1)}, u32[]{:S(2)}) copy-start(f32[3,512,1024]{2,1,0:T(8,128)S(1)} %get-tuple-element.12.weights) | copy-start | bytes 18874372
  19.1 1.1 %copy-start.5 = (bf16[3,256,1024]{2,1,0:T(8,128)(2,1)}, bf16[3,256,1024]{2,1,0:T(8,128)(2,1)S(1)}, u32[]{:S(2)}) copy-start(bf16[3,256,1024]{2,1,0:T(8,128)(2,1)S(1)} %get-tuple-element.13.hots) | copy-start | bytes 4718596
  23.7 20.7 %all-to-all-start.2 = ((f32[32,64,128]{2,1,0:T(8,128)}), f32[32,64,128]{2,1,0:T(8,128)S(1)}, u32[]{:S(2)}, u32[]{:S(2)}) async-start(f32[32,64,128]{2,1,0:T(8,128)} %bitcast.14), calls=%async_computation.2 | async-start | bytes 2097152 | tf_op jit(solution)/shard_map/all_to_all | solution.py:448
  29.7 22.0 %copy-start = (f32[128,64]{0,1:T(8,128)S(1)}, f32[128,64]{0,1:T(8,128)}, u32[]{:S(2)}) copy-start(f32[128,64]{0,1:T(8,128)} %param.20) | copy-start | bytes 98308
  29.7 22.0 %copy-start.3 = (s32[1,2,32]{2,1,0:T(2,128)S(1)}, s32[1,2,32]{2,1,0:T(2,128)}, u32[]{:S(2)}) copy-start(s32[1,2,32]{2,1,0:T(2,128)} %param.22) | copy-start | bytes 772
  44.4 22.4 %all-to-all-start.1 = ((f32[32,32,128]{2,1,0:T(8,128)}), f32[32,32,128]{2,1,0:T(8,128)S(1)}, u32[]{:S(2)}, u32[]{:S(2)}) async-start(f32[32,32,128]{2,1,0:T(8,128)} %bitcast.12), calls=%async_computation.1 | async-start | bytes 1048576 | tf_op jit(solution)/shard_map/all_to_all | solution.py:466
  51.8 11.8 %slice-start = ((s8[6291456]{0:T(1024)(128)(4,1)}), s8[4194304]{0:T(1024)(128)(4,1)S(1)}, s32[]{:S(2)}) async-start(s8[6291456]{0:T(1024)(128)(4,1)} %bitcast.30), calls=%async_computation.3 | async-start | bytes 8388608
  53.7 7.7 %collective-permute-start = (f32[128,128]{1,0:T(8,128)S(1)}, f32[128,128]{1,0:T(8,128)S(1)}, u32[]{:S(2)}, u32[]{:S(2)}) collective-permute-start(f32[128,128]{1,0:T(8,128)S(1)} %get-tuple-element.10), channel_id=1, source_target_pairs={{0,1},{1,2},{2,3},{4,5},{5,6},{6,7},{8,9},{9,10},{10,11},{12,13},{... | collective-permute-start | bytes 196616 | tf_op jit(solution)/shard_map/ppermute | solution.py:489
  57.2 6.4 %slice-start.1 = ((s8[6291456]{0:T(1024)(128)(4,1)}), s8[2097152]{0:T(1024)(128)(4,1)S(1)}, s32[]{:S(2)}) async-start(s8[6291456]{0:T(1024)(128)(4,1)} %bitcast.30), calls=%async_computation.4 | async-start | bytes 4194304
  57.2 6.4 %copy-start.6 = (bf16[3,256,1024]{2,1,0:T(8,128)(2,1)S(1)}, bf16[3,256,1024]{2,1,0:T(8,128)(2,1)}, u32[]{:S(2)}) copy-start(bf16[3,256,1024]{2,1,0:T(8,128)(2,1)} %copy-done.5) | copy-start | bytes 4718596
  57.2 6.4 %collective-permute-start.1 = (f32[128,128]{1,0:T(8,128)S(1)}, f32[128,128]{1,0:T(8,128)S(1)}, u32[]{:S(2)}, u32[]{:S(2)}) collective-permute-start(f32[128,128]{1,0:T(8,128)S(1)} %get-tuple-element.11), channel_id=1, source_target_pairs={{1,0},{2,1},{3,2},{5,4},{6,5},{7,6},{9,8},{10,9},{11,10},{13,12},{... | collective-permute-start | bytes 196616 | tf_op jit(solution)/shard_map/ppermute | solution.py:490
